TPU v7x, 32 devices: a whole 2x2x4 slice. The times are simulated.
32 devices in a mesh: dp: 32 (over z, y, x, core).
Axes of the slice: x: 2, y: 2, z: 4, core: 2. Of those that a mesh axis runs over, the one named last changes fastest.
Arguments:
- tokens: bfloat16 [24576, 768], P('dp'), may hold values from -6 to 6
- cotangent: bfloat16 [24576, 768], P('dp'), may hold values from -6 to 6
- lengths: int32 [24], replicated, may hold values from 1 to 2048, 24576 in all
- gain_norm1: bfloat16 [768], P('dp'), may hold values from 0.25 to 1.75
- gain_norm2: bfloat16 [768], P('dp'), may hold values from 0.25 to 1.75
- proj_in: bfloat16 [768, 2048], P('dp'), may hold values from -0.21875 to 0.21875
- out_proj: bfloat16 [768, 1024], P('dp'), may hold values from -0.5 to 0.5
- gate_blocks: bfloat16 [1024, 512], P('dp'), may hold values from -0.375 to 0.375
- conv_weight: bfloat16 [4, 1024], P(None, 'dp'), may hold values from -3 to 3
- conv_bias: bfloat16 [1024], P('dp'), may hold values from -3 to 3
- gate_bias: bfloat16 [2, 1024], P(None, 'dp'), may hold values from -4 to 4
- decay_param: bfloat16 [1024], P('dp'), may hold values from -11.6 to -3.8
- mlp_in: bfloat16 [2304, 1536], P('dp'), may hold values from -0.21875 to 0.21875
- mlp_down: bfloat16 [2304, 768], P('dp'), may hold values from -0.25 to 0.25
Outputs:
- output: bfloat16 [24576, 768], P('dp')
- grad_tokens: bfloat16 [24576, 768], P('dp')
- grad_gain_norm1: float32 [768], P('dp')
- grad_gain_norm2: float32 [768], P('dp')
- grad_proj_in: float32 [768, 2048], P('dp')
- grad_out_proj: float32 [768, 1024], P('dp')
- grad_gate_blocks: float32 [1024, 512], P('dp')
- grad_conv_weight: float32 [4, 1024], P(None, 'dp')
- grad_conv_bias: float32 [1024], P('dp')
- grad_gate_bias: float32 [2, 1024], P(None, 'dp')
- grad_decay_param: float32 [1024], P('dp')
- grad_mlp_in: float32 [2304, 1536], P('dp')
- grad_mlp_down: float32 [2304, 768], P('dp')
Inputs may be any that keep to these rules, and one draw needn't show every extreme that they name: Together the lengths fill all 24576 rows; the longest is exactly 2048.
All inputs are finite; a program needn't handle non-finite values.
Results may differ from a plain program's by a relative error of at most 0.009.
Values may be sent and summed in bfloat16 or wider, within the bound.
A program may use at most 192 MiB of HBM per device.

v0:
```python
from functools import partial

import jax
import jax.numpy as jnp
from jax import lax
from jax.sharding import PartitionSpec as P

EPSILON = 1e-06


def from_behind(x, axis, by):
    size = lax.axis_size(axis)
    pairs = [(i, i + by) for i in range(size) if 0 <= i + by < size]
    return lax.ppermute(x, axis, pairs)


def prefix(part, axis, combine, identity, reverse):
    count = lax.axis_size(axis)
    place = lax.axis_index(axis)
    ahead = count - 1 - place if reverse else place
    gathered = jax.tree.map(lambda a: lax.all_gather(a, axis), part)
    state = jax.tree.map(lambda a, e: jnp.zeros_like(a) + jnp.asarray(e, a.dtype), part, identity)

    def one(lap, state):
        source = count - 1 - lap if reverse else lap
        return combine(
            state, jax.tree.map(lambda a: lax.dynamic_index_in_dim(a, source, 0, False), gathered)
        )

    return lax.fori_loop(0, ahead, one, state)


def rms_scale(values, gain_row):
    inverse = lax.rsqrt(jnp.mean(values * values, axis=-1, keepdims=True) + EPSILON)
    return values * inverse * gain_row


def combine_steps(earlier, later):
    return (earlier[0] * later[0], later[0] * earlier[1] + later[1])


def smooth_gelu(inputs):
    return jax.nn.gelu(inputs, approximate=True)


def glu_piece(gate_pre, up_value):
    return smooth_gelu(gate_pre) * up_value


def gate_math(gate_pre, bias_rows, decay_vec, coded_rows, fresh_row):
    tok_rows, rnn_width = coded_rows.shape
    block_size = gate_pre.shape[2] // 2
    gate_x = jax.nn.sigmoid(gate_pre[:, :, :block_size].reshape(tok_rows, rnn_width) + bias_rows[0])
    gate_a = jax.nn.sigmoid(gate_pre[:, :, block_size:].reshape(tok_rows, rnn_width) + bias_rows[1])
    log_a = -8.0 * gate_a * jax.nn.softplus(decay_vec)
    factor = jnp.where(fresh_row, 0.0, jnp.exp(log_a))
    scale_term = jnp.where(fresh_row, 1.0, jnp.sqrt(-jnp.expm1(2.0 * log_a)))
    return (factor, scale_term * gate_x * coded_rows)


def per_device(
    tokens,
    cotangent,
    lengths,
    gain_norm1,
    gain_norm2,
    proj_in,
    out_proj,
    gate_blocks,
    conv_weight,
    conv_bias,
    gate_bias,
    decay_param,
    mlp_in,
    mlp_down,
):
    tok_rows, model_width = tokens.shape
    conv_taps = conv_weight.shape[0]
    reach_back = conv_taps - 1
    first_row = lax.axis_index("dp") * tok_rows
    places = first_row + jnp.arange(-reach_back, tok_rows, dtype=jnp.int32)
    bounds = jnp.cumsum(lengths)
    labels = jnp.sum((places[:, None] >= bounds[None, :]).astype(jnp.int32), axis=1)
    labels = jnp.where(places < 0, -1, labels)
    own_label = labels[reach_back:]
    fresh_row = (own_label != labels[reach_back - 1 : reach_back - 1 + tok_rows])[:, None]
    tap_masks = [
        (labels[reach_back - offset : reach_back - offset + tok_rows] == own_label)[:, None].astype(
            jnp.float32
        )
        for offset in range(conv_taps)
    ]
    gathered = (
        lax.all_gather(proj_in, "dp", axis=0, tiled=True),
        lax.all_gather(out_proj, "dp", axis=0, tiled=True),
        lax.all_gather(gate_blocks, "dp", axis=0, tiled=True),
        lax.all_gather(gain_norm1, "dp", axis=0, tiled=True),
        lax.all_gather(gain_norm2, "dp", axis=0, tiled=True),
        lax.all_gather(conv_weight, "dp", axis=1, tiled=True),
        lax.all_gather(conv_bias, "dp", axis=0, tiled=True),
        lax.all_gather(gate_bias, "dp", axis=1, tiled=True),
        lax.all_gather(decay_param, "dp", axis=0, tiled=True),
    )
    w_proj, w_out, w_gates = (gathered[0], gathered[1], gathered[2])
    gain_one = gathered[3].astype(jnp.float32)
    gain_two = gathered[4].astype(jnp.float32)
    w_conv = gathered[5].astype(jnp.float32)
    b_conv = gathered[6].astype(jnp.float32)
    b_gates = gathered[7].astype(jnp.float32)
    w_decay = gathered[8].astype(jnp.float32)
    rnn_width = w_conv.shape[1]
    w_mlp, w_down = (
        lax.all_gather(mlp_in, "dp", axis=0, tiled=True),
        lax.all_gather(mlp_down, "dp", axis=0, tiled=True),
    )
    residual = tokens.astype(jnp.float32)
    normed_one, norm_one_back = jax.vjp(rms_scale, residual, gain_one)
    u_one = normed_one.astype(jnp.bfloat16)
    projected = jnp.dot(u_one, w_proj, preferred_element_type=jnp.float32)
    branch_x = projected[:, :rnn_width].astype(jnp.bfloat16)
    branch_y = projected[:, rnn_width:]
    rim_rows = from_behind(branch_x[tok_rows - reach_back :], "dp", 1)
    padded = jnp.concatenate([rim_rows, branch_x], axis=0)
    conv_sum = jnp.zeros((tok_rows, rnn_width), jnp.float32) + b_conv
    for offset in range(conv_taps):
        conv_sum = (
            conv_sum
            + w_conv[offset]
            * padded[reach_back - offset : reach_back - offset + tok_rows].astype(jnp.float32)
            * tap_masks[offset]
        )
    coded_rows = conv_sum.astype(jnp.bfloat16)
    block_size = w_gates.shape[1] // 2
    head_count = rnn_width // block_size
    blocks_w = w_gates.reshape(head_count, block_size, 2 * block_size)
    coded_heads = coded_rows.reshape(tok_rows, head_count, block_size)
    gate_pre = jnp.einsum("thi,hij->thj", coded_heads, blocks_w, preferred_element_type=jnp.float32)
    gate_fn = partial(gate_math, fresh_row=fresh_row)
    (factor, drive_term), gate_back = jax.vjp(
        gate_fn, gate_pre, b_gates, w_decay, coded_rows.astype(jnp.float32)
    )
    prefix_a, local_h = lax.associative_scan(combine_steps, (factor, drive_term), axis=0)
    unit_pair = (jnp.ones((rnn_width,), jnp.float32), jnp.zeros((rnn_width,), jnp.float32))
    carry_unused, carry_h = prefix(
        (prefix_a[-1], local_h[-1]), "dp", combine_steps, unit_pair, False
    )
    state_rows = local_h + prefix_a * carry_h[None, :]
    y_branch_act, y_back = jax.vjp(smooth_gelu, branch_y)
    mixed_rows = (state_rows * y_branch_act).astype(jnp.bfloat16)
    middle = residual + jnp.einsum(
        "tr,dr->td", mixed_rows, w_out, preferred_element_type=jnp.float32
    )
    normed_two, norm_two_back = jax.vjp(rms_scale, middle, gain_two)
    u_two = normed_two.astype(jnp.bfloat16)
    gate_val = jnp.einsum(
        "td,fd->tf", u_two, w_mlp[:, :model_width], preferred_element_type=jnp.float32
    )
    up_val = jnp.einsum(
        "td,fd->tf", u_two, w_mlp[:, model_width:], preferred_element_type=jnp.float32
    )
    glu_value, glu_back = jax.vjp(glu_piece, gate_val, up_val)
    hidden = glu_value.astype(jnp.bfloat16)
    output = (middle + jnp.dot(hidden, w_down, preferred_element_type=jnp.float32)).astype(
        jnp.bfloat16
    )
    w_proj, w_out, w_gates = (
        lax.all_gather(proj_in, "dp", axis=0, tiled=True),
        lax.all_gather(out_proj, "dp", axis=0, tiled=True),
        lax.all_gather(gate_blocks, "dp", axis=0, tiled=True),
    )
    w_mlp, w_down = (
        lax.all_gather(mlp_in, "dp", axis=0, tiled=True),
        lax.all_gather(mlp_down, "dp", axis=0, tiled=True),
    )
    blocks_w = w_gates.reshape(head_count, block_size, 2 * block_size)
    d_hidden = jnp.einsum("td,fd->tf", cotangent, w_down, preferred_element_type=jnp.float32)
    d_gate_f, d_up_f = glu_back(d_hidden)
    d_gate = d_gate_f.astype(jnp.bfloat16)
    d_up = d_up_f.astype(jnp.bfloat16)
    feed_sum = None
    d_u_two = jnp.einsum(
        "tf,fd->td", d_gate, w_mlp[:, :model_width], preferred_element_type=jnp.float32
    )
    d_u_two = d_u_two + jnp.einsum(
        "tf,fd->td", d_up, w_mlp[:, model_width:], preferred_element_type=jnp.float32
    )
    d_norm_mid, d_gain_two = norm_two_back(d_u_two)
    d_middle = cotangent.astype(jnp.float32) + d_norm_mid
    d_branch = d_middle.astype(jnp.bfloat16)
    d_mixed = jnp.dot(d_branch, w_out, preferred_element_type=jnp.float32)
    d_state = d_mixed * y_branch_act
    d_branch_y = y_back(d_mixed * state_rows)[0].astype(jnp.bfloat16)
    ahead_factor = jnp.concatenate([factor[1:], jnp.ones((1, rnn_width), jnp.float32)], axis=0)
    back_prod, local_g = lax.associative_scan(
        combine_steps, (ahead_factor, d_state), reverse=True, axis=0
    )
    carry_skip, carry_q = prefix(
        (factor[0] * back_prod[0], factor[0] * local_g[0]), "dp", combine_steps, unit_pair, True
    )
    adjoint = local_g + back_prod * carry_q[None, :]
    before = jnp.concatenate([carry_h[None, :], state_rows[:-1]], axis=0)
    d_pre_f, d_shift, d_decay, d_coded_part = gate_back((adjoint * before, adjoint))
    d_pre = d_pre_f.astype(jnp.bfloat16)
    d_coded = d_coded_part + jnp.einsum(
        "thj,hij->thi", d_pre, blocks_w, preferred_element_type=jnp.float32
    ).reshape(tok_rows, rnn_width)
    gate_grad = jnp.einsum(
        "thi,thj->hij", coded_heads, d_pre, preferred_element_type=jnp.float32
    ).reshape(rnn_width, 2 * block_size)
    spread = jnp.zeros((tok_rows + reach_back, rnn_width), jnp.float32)
    tap_grads = []
    for offset in range(conv_taps):
        spread = spread + jnp.pad(
            w_conv[offset] * tap_masks[offset] * d_coded, ((reach_back - offset, offset), (0, 0))
        )
        tap_grads.append(
            jnp.sum(
                d_coded
                * tap_masks[offset]
                * padded[reach_back - offset : reach_back - offset + tok_rows].astype(jnp.float32),
                axis=0,
            )
        )
    d_conv_w = jnp.stack(tap_grads, axis=0)
    d_conv_b = jnp.sum(d_coded, axis=0)
    back_rim = from_behind(spread[:reach_back], "dp", -1)
    d_branch_x = (
        spread[reach_back:] + jnp.pad(back_rim, ((tok_rows - reach_back, 0), (0, 0)))
    ).astype(jnp.bfloat16)
    d_projected = jnp.concatenate([d_branch_x, d_branch_y], axis=1)
    d_u_one = jnp.einsum("tk,dk->td", d_projected, w_proj, preferred_element_type=jnp.float32)
    d_norm_in, d_gain_one = norm_one_back(d_u_one)
    grad_tokens = (d_middle + d_norm_in).astype(jnp.bfloat16)
    part_gate = jnp.einsum("tf,td->fd", d_gate, u_two, preferred_element_type=jnp.float32)
    part_up = jnp.einsum("tf,td->fd", d_up, u_two, preferred_element_type=jnp.float32)
    part_down = jnp.einsum("tf,td->fd", hidden, cotangent, preferred_element_type=jnp.float32)
    feed_sum = lax.psum_scatter(
        jnp.concatenate([part_gate, part_up, part_down], axis=1),
        "dp",
        scatter_dimension=0,
        tiled=True,
    )
    part_proj = jnp.einsum("td,tk->dk", u_one, d_projected, preferred_element_type=jnp.float32)
    part_out = jnp.einsum("td,tr->dr", d_branch, mixed_rows, preferred_element_type=jnp.float32)
    rec_sum = lax.psum_scatter(
        jnp.concatenate([part_proj, part_out], axis=1), "dp", scatter_dimension=0, tiled=True
    )
    channel_sums = (
        lax.psum_scatter(d_gain_one, "dp", scatter_dimension=0, tiled=True),
        lax.psum_scatter(d_gain_two, "dp", scatter_dimension=0, tiled=True),
        lax.psum_scatter(d_conv_w, "dp", scatter_dimension=1, tiled=True),
        lax.psum_scatter(d_conv_b, "dp", scatter_dimension=0, tiled=True),
        lax.psum_scatter(d_shift, "dp", scatter_dimension=1, tiled=True),
        lax.psum_scatter(d_decay, "dp", scatter_dimension=0, tiled=True),
        lax.psum_scatter(gate_grad, "dp", scatter_dimension=0, tiled=True),
    )
    return (
        output,
        grad_tokens,
        channel_sums[0],
        channel_sums[1],
        rec_sum[:, : 2 * rnn_width],
        rec_sum[:, 2 * rnn_width :],
        channel_sums[6],
        channel_sums[2],
        channel_sums[3],
        channel_sums[4],
        channel_sums[5],
        feed_sum[:, : 2 * model_width],
        feed_sum[:, 2 * model_width :],
    )


def solution(mesh):
    placed = (
        P("dp", None),
        P("dp", None),
        P(),
        P("dp"),
        P("dp"),
        P("dp", None),
        P("dp", None),
        P("dp", None),
        P(None, "dp"),
        P("dp"),
        P(None, "dp"),
        P("dp"),
        P("dp", None),
        P("dp", None),
    )
    return jax.shard_map(
        per_device,
        mesh=mesh,
        in_specs=placed,
        out_specs=(
            P("dp", None),
            P("dp", None),
            P("dp"),
            P("dp"),
            P("dp", None),
            P("dp", None),
            P("dp", None),
            P(None, "dp"),
            P("dp"),
            P(None, "dp"),
            P("dp"),
            P("dp", None),
            P("dp", None),
        ),
        check_vma=False,
    )
```

profile of v0, /device:TPU:0, one launch (start us, length us, event | category | flops | bytes accessed | tf_op | source)
XLA Modules:
  0.0 1966.2 jit_solution(17033855323244369)
XLA Ops:
  15.6 42.5 %all-reduce.92 = (bf16[1024]{0:T(1024)(128)(2,1)S(1)}, bf16[768]{0:T(1024)(128)(2,1)S(1)}, bf16[1024]{0:T(1024)(128)(2,1)S(1)}, bf16[768]{0:T(1024)(128)(2,1)S(1)}) all-reduce(bf16[1024]{0:T(1024)(128)(2,1)S(1)} %dynamic-update-slice.2, bf16[768]{0:T(1024)(128)(2,1)S(1)} %dynamic-update-slice.1, ...), channel_id=1, replica_groups=mesh['dp'=32] {'dp'}, use_global_device_ids=true, to_apply=%add.85 | all-reduce | flops 3584 | bytes 14336
  59.5 40.1 %all-gather = bf16[32,32,4]{1,2,0:T(4,128)(2,1)S(1)} all-gather(bf16[1,32,4]{1,2,0:T(4,128)(2,1)S(1)} %bitcast.160), channel_id=1, replica_groups=mesh['dp'=32] {'dp'}, dimensions={0}, use_global_device_ids=true | all-gather | bytes 8448 | tf_op jit(solution)/shard_map/all_gather | solution.py:99
  99.8 36.4 %all-gather.1 = bf16[32,32,2]{1,2,0:T(2,128)(2,1)S(1)} all-gather(bf16[1,32,2]{1,2,0:T(2,128)(2,1)S(1)} %bitcast.162), channel_id=1, replica_groups=mesh['dp'=32] {'dp'}, dimensions={0}, use_global_device_ids=true | all-gather | bytes 4224 | tf_op jit(solution)/shard_map/all_gather | solution.py:101
  169.3 7.6 convert_multiply_fusion.5
  177.0 7.8 slice.684
  184.8 7.6 slice.683
  320.7 7.8 slice.748
  338.4 7.6 slice.773
  346.1 7.7 slice.782
  353.8 7.7 slice.775
  443.7 9.6 pad.289
  475.3 9.7 pad.288
  485.8 38.3 %all-gather.2 = f32[32,1,1024]{2,1,0:T(1,128)S(1)} all-gather(f32[1,1,1024]{2,1,0:T(1,128)S(1)} %add_bitcast_fusion.1), channel_id=1, replica_groups=mesh['dp'=32] {'dp'}, dimensions={0}, use_global_device_ids=true | all-gather | bytes 135168 | tf_op jit(solution)/shard_map/all_gather | solution.py:21
  524.1 9.8 pad.271
  536.7 9.5 pad.270
  547.0 37.1 %all-gather.3 = f32[32,1,1024]{2,1,0:T(1,128)S(1)} all-gather(f32[1,1,1024]{2,1,0:T(1,128)S(1)} %add_bitcast_fusion), channel_id=1, replica_groups=mesh['dp'=32] {'dp'}, dimensions={0}, use_global_device_ids=true | all-gather | bytes 135168 | tf_op jit(solution)/shard_map/all_gather | solution.py:21
  584.1 13.1 slice.774
  597.2 12.8 slice.783
  610.0 12.8 slice.776
  622.8 8.9 multiply_convert_fusion.2
  638.1 8.1 fusion.126
  646.2 8.3 fusion.35
  654.5 12.9 fusion.6
  667.5 7.7 fusion.33
  689.2 7.7 slice.779
  704.5 12.8 slice.780
  717.3 12.8 slice.778
  849.6 7.9 slice.845
  859.6 13.2 slice.846
  968.1 9.7 pad.306
  977.8 9.7 pad.307
  992.9 9.7 pad.324
  1002.6 9.7 pad.325
  1018.5 24.7 %rev.8 = f32[768,1024]{1,0:T(8,128)} reverse(f32[768,1024]{1,0:T(8,128)} %add.665), dimensions={0} | reverse | bytes 6291456 | tf_op jit(solution)/shard_map/rev | solution.py:194
  1043.2 24.8 %rev.9 = f32[768,1024]{1,0:T(8,128)} reverse(f32[768,1024]{1,0:T(8,128)} %add.674), dimensions={0} | reverse | bytes 6291456 | tf_op jit(solution)/shard_map/rev | solution.py:194
  1068.0 39.9 %all-gather.4 = f32[32,1,1024]{2,1,0:T(1,128)S(1)} all-gather(f32[1,1,1024]{2,1,0:T(1,128)S(1)} %get-tuple-element.281), channel_id=1, replica_groups=mesh['dp'=32] {'dp'}, dimensions={0}, use_global_device_ids=true | all-gather | bytes 135168 | tf_op jit(solution)/shard_map/all_gather | solution.py:21
  1107.9 37.0 %all-gather.5 = f32[32,1,1024]{2,1,0:T(1,128)S(1)} all-gather(f32[1,1,1024]{2,1,0:T(1,128)S(1)} %get-tuple-element.280), channel_id=1, replica_groups=mesh['dp'=32] {'dp'}, dimensions={0}, use_global_device_ids=true | all-gather | bytes 135168 | tf_op jit(solution)/shard_map/all_gather | solution.py:21
  1146.8 10.0 fusion.109
  1170.0 10.0 fusion.14
  1216.0 7.6 pad_maximum_fusion
  1223.6 22.1 %copy.147 = f32[2304,2304]{1,0:T(8,128)} copy(f32[2304,2304]{0,1:T(8,128)} %pad_maximum_fusion) | data formatting | bytes 42467328
  1252.4 7.9 add_convert_fusion.1
  1270.4 38.8 %all-reduce.91 = (f32[768]{0:T(1024)S(1)}, f32[768]{0:T(1024)S(1)}, f32[1024]{0:T(1024)S(1)}, f32[1024]{0:T(1024)S(1)}) all-reduce(f32[768]{0:T(1024)S(1)} %get-tuple-element.213, f32[768]{0:T(1024)S(1)} %copy-done.120, f32[1024]{0:T(1024)S(1)} %get-tuple-element.215, f32[1024]{0:T(1024)S(1)} %fusion.98), channel_id=2, replica_groups=mesh['dp'=32] {'dp'}, use_global_device_ids=true, to_apply=%region_11.12.clone | all-reduce | flops 3584 | bytes 28672
  1311.5 13.0 reduce-scatter.18.cloned.1.call-done
  1325.9 130.7 %reduce-scatter.16.cloned.1.call-done = f32[32,4]{1,0:T(8,128)} async-done(((f32[1024,4]{1,0:T(8,128)}), f32[32,4]{1,0:T(8,128)}) %reduce-scatter.16.cloned.1.call-update) | async-done | bytes 528
  1458.0 136.0 %reduce-scatter.12.cloned.1.call-done = f32[24,3072]{1,0:T(8,128)} async-done(((f32[768,3072]{1,0:T(8,128)}), f32[24,3072]{1,0:T(8,128)}) %reduce-scatter.12.cloned.1.call-update) | async-done | bytes 294928 | tf_op jit(solution)/shard_map/reduce_scatter | solution.py:245
  1597.1 223.4 %reduce-scatter.20.cloned.1.call-done = f32[72,2304]{1,0:T(8,128)} async-done(((f32[2304,2304]{1,0:T(8,128)}), f32[72,2304]{1,0:T(8,128)}) %reduce-scatter.20.cloned.1.call-update) | async-done | bytes 663568
  1823.9 135.2 %reduce-scatter.14.cloned.1.call-done = f32[32,512]{1,0:T(8,128)} async-done(((f32[1024,512]{1,0:T(8,128)}), f32[32,512]{1,0:T(8,128)}) %reduce-scatter.14.cloned.1.call-update) | async-done | bytes 65552 | tf_op jit(solution)/shard_map/reduce_scatter | solution.py:255
  (731 shorter events, 624.8 us)
Async XLA Ops:
  7.2 51.8 %copy-start.122 = (s32[24]{0:T(128)S(1)}, s32[24]{0:T(128)}, u32[]{:S(2)}) copy-start(s32[24]{0:T(128)} %param.20) | copy-start | bytes 292
  7.2 52.3 %copy-start.121 = (bf16[4,32]{1,0:T(4,128)(2,1)S(1)}, bf16[4,32]{1,0:T(4,128)(2,1)}, u32[]{:S(2)}) copy-start(bf16[4,32]{1,0:T(4,128)(2,1)} %param.26) | copy-start | bytes 772
  7.2 92.6 %copy-start.123 = (bf16[2,32]{1,0:T(2,128)(2,1)S(1)}, bf16[2,32]{1,0:T(2,128)(2,1)}, u32[]{:S(2)}) copy-start(bf16[2,32]{1,0:T(2,128)(2,1)} %param.28) | copy-start | bytes 388
  7.2 129.2 %all-gather.12.cloned.1.call-start = ((), (), s32[]{:S(2)}) async-start(), calls=%async_computation.5 | async-start | bytes 3244032 | tf_op jit(solution)/shard_map/all_gather | solution.py:94
  7.9 148.1 %all-gather.14.cloned.1.call-start = ((), (), s32[]{:S(2)}) async-start(), calls=%async_computation.6 | async-start | bytes 1081344 | tf_op jit(solution)/shard_map/all_gather | solution.py:96
  8.7 623.0 %all-gather.16.cloned.1.call-start = ((), (), s32[]{:S(2)}) async-start(), calls=%async_computation.7 | async-start | bytes 1622016 | tf_op jit(solution)/shard_map/all_gather | solution.py:95
  9.4 628.6 %all-gather.20.cloned.1.call-start = ((), (), s32[]{:S(2)}) async-start(), calls=%async_computation.9 | async-start | bytes 3649536 | tf_op jit(solution)/shard_map/all_gather | solution.py:114
  10.0 636.2 %all-gather.18.cloned.1.call-start = ((), (), s32[]{:S(2)}) async-start(), calls=%async_computation.8 | async-start | bytes 7299072 | tf_op jit(solution)/shard_map/all_gather | solution.py:113
  10.6 1313.9 %reduce-scatter.18.cloned.1.call-start = ((), (), s32[]{:S(2)}) async-start(), calls=%async_computation.13 | async-start | bytes 540672
  12.2 130.9 %copy-start.20 = (bf16[768,768]{0,1:T(8,128)(2,1)}, bf16[768,768]{0,1:T(8,128)(2,1)S(1)}, u32[]{:S(2)}) copy-start(bf16[768,768]{0,1:T(8,128)(2,1)S(1)} %copy.113) | copy-start | bytes 3538948
  58.1 89.1 %copy-start.118 = (bf16[1024]{0:T(1024)(128)(2,1)}, bf16[1024]{0:T(1024)(128)(2,1)S(1)}, u32[]{:S(2)}) copy-start(bf16[1024]{0:T(1024)(128)(2,1)S(1)} %get-tuple-element.241) | copy-start | bytes 6148
  58.1 85.0 %copy-start.92 = (f32[768]{0:T(1024)}, f32[768]{0:T(1024)S(1)}, u32[]{:S(2)}) copy-start(f32[768]{0:T(1024)S(1)} %convert_element_type.116) | copy-start | bytes 9220
  59.0 84.2 %copy-start.94 = (f32[768]{0:T(1024)}, f32[768]{0:T(1024)S(1)}, u32[]{:S(2)}) copy-start(f32[768]{0:T(1024)S(1)} %fusion.103) | copy-start | bytes 9220
  59.5 92.0 %copy-start.61 = (f32[768]{0:T(1024)}, f32[768]{0:T(1024)S(1)}, u32[]{:S(2)}) copy-start(f32[768]{0:T(1024)S(1)} %get-tuple-element.360) | copy-start | bytes 9220
  59.5 92.0 %copy-start.63 = (f32[768]{0:T(1024)}, f32[768]{0:T(1024)S(1)}, u32[]{:S(2)}) copy-start(f32[768]{0:T(1024)S(1)} %get-tuple-element.361) | copy-start | bytes 9220
  59.5 92.0 %copy-start.65 = (f32[768]{0:T(1024)}, f32[768]{0:T(1024)S(1)}, u32[]{:S(2)}) copy-start(f32[768]{0:T(1024)S(1)} %get-tuple-element.362) | copy-start | bytes 9220
  59.5 109.9 %copy-start.90 = (pred[768]{0:T(1024)(128)(4,1)}, pred[768]{0:T(1024)(128)(4,1)S(1)}, u32[]{:S(2)}) copy-start(pred[768]{0:T(1024)(128)(4,1)S(1)} %get-tuple-element.363) | copy-start | bytes 2308
  99.7 51.7 %copy-start.75 = (f32[1,1024]{1,0:T(1,128)}, f32[1,1024]{1,0:T(1,128)S(1)}, u32[]{:S(2)}) copy-start(f32[1,1024]{1,0:T(1,128)S(1)} %get-tuple-element.350) | copy-start | bytes 12292
  99.7 51.7 %copy-start.77 = (f32[1,1024]{1,0:T(1,128)}, f32[1,1024]{1,0:T(1,128)S(1)}, u32[]{:S(2)}) copy-start(f32[1,1024]{1,0:T(1,128)S(1)} %get-tuple-element.351) | copy-start | bytes 12292
  99.7 51.7 %copy-start.79 = (f32[1,1024]{1,0:T(1,128)}, f32[1,1024]{1,0:T(1,128)S(1)}, u32[]{:S(2)}) copy-start(f32[1,1024]{1,0:T(1,128)S(1)} %get-tuple-element.352) | copy-start | bytes 12292
  99.7 51.7 %copy-start.81 = (f32[1,1024]{1,0:T(1,128)}, f32[1,1024]{1,0:T(1,128)S(1)}, u32[]{:S(2)}) copy-start(f32[1,1024]{1,0:T(1,128)S(1)} %get-tuple-element.353) | copy-start | bytes 12292
  136.3 33.0 %copy-start.57 = (f32[1,1024]{1,0:T(1,128)}, f32[1,1024]{1,0:T(1,128)S(1)}, u32[]{:S(2)}) copy-start(f32[1,1024]{1,0:T(1,128)S(1)} %get-tuple-element.358) | copy-start | bytes 12292
  136.3 33.0 %copy-start.59 = (f32[1,1024]{1,0:T(1,128)}, f32[1,1024]{1,0:T(1,128)S(1)}, u32[]{:S(2)}) copy-start(f32[1,1024]{1,0:T(1,128)S(1)} %get-tuple-element.359) | copy-start | bytes 12292
  144.8 6.6 collective-permute-start
  361.5 22.7 %copy-start.113 = (f32[1,1024]{1,0:T(1,128)S(1)}, f32[1,1024]{1,0:T(1,128)}, u32[]{:S(2)}) copy-start(f32[1,1024]{1,0:T(1,128)} %slice.919) | copy-start | bytes 12292
  368.8 23.6 %copy-start.108 = (f32[1,1024]{1,0:T(1,128)S(1)}, f32[1,1024]{1,0:T(1,128)}, u32[]{:S(2)}) copy-start(f32[1,1024]{1,0:T(1,128)} %slice.889) | copy-start | bytes 12292
  485.0 48.8 %copy-start.97 = (f32[1,1024]{1,0:T(1,128)S(1)}, f32[1,1024]{1,0:T(1,128)}, u32[]{:S(2)}) copy-start(f32[1,1024]{1,0:T(1,128)} %slice.886) | copy-start | bytes 12292
  849.5 23.2 %copy-start.70 = (f32[3,1024]{1,0:T(4,128)S(1)}, f32[3,1024]{1,0:T(4,128)}, u32[]{:S(2)}) copy-start(f32[3,1024]{1,0:T(4,128)} %slice.825) | copy-start | bytes 36868
  849.5 23.2 %copy-start.71 = (f32[3,1024]{1,0:T(4,128)S(1)}, f32[3,1024]{1,0:T(4,128)}, u32[]{:S(2)}) copy-start(f32[3,1024]{1,0:T(4,128)} %slice.821) | copy-start | bytes 36868
  849.5 23.2 %copy-start.72 = (f32[3,1024]{1,0:T(4,128)S(1)}, f32[3,1024]{1,0:T(4,128)}, u32[]{:S(2)}) copy-start(f32[3,1024]{1,0:T(4,128)} %slice.823) | copy-start | bytes 36868
  849.5 23.2 %copy-start.73 = (f32[3,1024]{1,0:T(4,128)S(1)}, f32[3,1024]{1,0:T(4,128)}, u32[]{:S(2)}) copy-start(f32[3,1024]{1,0:T(4,128)} %slice.822) | copy-start | bytes 36868
  849.5 23.4 %copy-start.89 = (f32[2,1024]{1,0:T(2,128)S(1)}, f32[2,1024]{1,0:T(2,128)}, u32[]{:S(2)}) copy-start(f32[2,1024]{1,0:T(2,128)} %slice.831) | copy-start | bytes 24580
  849.5 23.5 %copy-start.117 = (f32[1,1024]{1,0:T(1,128)S(1)}, f32[1,1024]{1,0:T(1,128)}, u32[]{:S(2)}) copy-start(f32[1,1024]{1,0:T(1,128)} %slice.983) | copy-start | bytes 12292
  849.6 23.5 %copy-start.116 = (f32[1,1024]{1,0:T(1,128)S(1)}, f32[1,1024]{1,0:T(1,128)}, u32[]{:S(2)}) copy-start(f32[1,1024]{1,0:T(1,128)} %slice.955) | copy-start | bytes 12292
  849.6 23.6 %copy-start.52 = (f32[5,1024]{1,0:T(8,128)S(1)}, f32[5,1024]{1,0:T(8,128)}, u32[]{:S(2)}) copy-start(f32[5,1024]{1,0:T(8,128)} %slice.814) | copy-start | bytes 61444
  849.6 23.6 %copy-start.54 = (f32[5,1024]{1,0:T(8,128)S(1)}, f32[5,1024]{1,0:T(8,128)}, u32[]{:S(2)}) copy-start(f32[5,1024]{1,0:T(8,128)} %slice.833) | copy-start | bytes 61444
  849.6 24.2 %copy-start.115 = (f32[1,1024]{1,0:T(1,128)S(1)}, f32[1,1024]{1,0:T(1,128)}, u32[]{:S(2)}) copy-start(f32[1,1024]{1,0:T(1,128)} %slice.982) | copy-start | bytes 12292
  1043.2 103.5 %copy-start.1 = (f32[768,1024]{1,0:T(8,128)S(1)}, f32[768,1024]{1,0:T(8,128)}, u32[]{:S(2)}) copy-start(f32[768,1024]{1,0:T(8,128)} %copy-done) | copy-start | bytes 9437188
  1043.2 103.5 %copy-start.56 = (f32[1024]{0:T(1024)S(1)}, f32[1024]{0:T(1024)}, u32[]{:S(2)}) copy-start(f32[1024]{0:T(1024)} %copy-done.55) | copy-start | bytes 12292
  1043.2 103.5 %copy-start.58 = (f32[1,1024]{1,0:T(1,128)S(1)}, f32[1,1024]{1,0:T(1,128)}, u32[]{:S(2)}) copy-start(f32[1,1024]{1,0:T(1,128)} %copy-done.57) | copy-start | bytes 12292
  1043.2 103.5 %copy-start.60 = (f32[1,1024]{1,0:T(1,128)S(1)}, f32[1,1024]{1,0:T(1,128)}, u32[]{:S(2)}) copy-start(f32[1,1024]{1,0:T(1,128)} %copy-done.59) | copy-start | bytes 12292
  1043.2 103.5 %copy-start.91 = (pred[768]{0:T(1024)(128)(4,1)S(1)}, pred[768]{0:T(1024)(128)(4,1)}, u32[]{:S(2)}) copy-start(pred[768]{0:T(1024)(128)(4,1)} %copy-done.90) | copy-start | bytes 2308
  1043.2 103.5 %copy-start.96 = (f32[1024]{0:T(1024)S(1)}, f32[1024]{0:T(1024)}, u32[]{:S(2)}) copy-start(f32[1024]{0:T(1024)} %get-tuple-element.364) | copy-start | bytes 12292
  1188.4 3.8 collective-permute-start.1
  1190.9 265.7 %reduce-scatter.16.cloned.1.call-start = ((), (), s32[]{:S(2)}) async-start(), calls=%async_computation.12 | async-start | bytes 540672
  1192.1 401.9 %reduce-scatter.12.cloned.1.call-start = ((), (), s32[]{:S(2)}) async-start(), calls=%async_computation.10 | async-start | bytes 9732096 | tf_op jit(solution)/shard_map/reduce_scatter | solution.py:245
  1203.5 617.0 %reduce-scatter.20.cloned.1.call-start = ((), (), s32[]{:S(2)}) async-start(), calls=%async_computation.14 | async-start | bytes 21897216
  1245.8 713.3 %reduce-scatter.14.cloned.1.call-start = ((), (), s32[]{:S(2)}) async-start(), calls=%async_computation.11 | async-start | bytes 2162688 | tf_op jit(solution)/shard_map/reduce_scatter | solution.py:255
  (96 other events, 677.2 us)
Sparse Core Ops, SparseCore 0:
  10.9 61.7 all-gather.11
  75.5 52.5 all-gather.13
  131.0 53.8 all-gather.15
  187.6 58.9 all-gather.19
  249.3 71.2 all-gather.17
  1191.0 133.4 reduce-scatter.17
  1326.8 129.7 reduce-scatter.15
  1462.5 131.4 reduce-scatter.11
  1601.5 218.9 reduce-scatter.19
  1823.2 135.8 reduce-scatter.13
where the time goes:
time: 1990 us; the launch traced here: 1970 us
  local copies, waits for them, and re-layouts  681 us (34%)
  waiting for transfers between devices  642 us (32%)
  blocking collectives  310 us (16%)
  other arithmetic  213 us (11%)
  matrix products  98.7 us (5%)
    unnamed x13, waiting for transfers between devices  370 us
    slice x69, local copies, waits for them, and re-layouts, per_device(): lax.associative_scan(combine_steps, (ahead_factor, d_state), reverse=True...  227 us
    all_gather x4, blocking collectives, prefix(): gathered = jax.tree.map(lambda a: lax.all_gather(a, axis), part)  152 us
    slice x64, local copies, waits for them, and re-layouts, per_device(): lax.associative_scan(combine_steps, (factor, drive_term), axis=0)  141 us
    reduce_scatter x1, waiting for transfers between devices, per_device(): lax.psum_scatter(jnp.concatenate([part_proj, part_out], axis=1), 'dp', sc...  136 us
    reduce_scatter x1, waiting for transfers between devices, per_device(): lax.psum_scatter(gate_grad, 'dp', scatter_dimension=0, tiled=True)  135 us
    pad x34, local copies, waits for them, and re-layouts, per_device(): lax.associative_scan(combine_steps, (factor, drive_term), axis=0)  91.9 us
    pad x34, local copies, waits for them, and re-layouts, per_device(): lax.associative_scan(combine_steps, (ahead_factor, d_state), reverse=True...  86.1 us
  transfers between devices with their start and end apart: 12, of which 5 were waited for; matrix products, arithmetic and copies ran while one was open for 26% of the time, Pallas kernels for 0%

commit v1 on v0

--- a/solution.py
+++ b/solution.py
@@ -1,11 +1,1138 @@
-from functools import partial
+import functools
 
 import jax
 import jax.numpy as jnp
 from jax import lax
+from jax.experimental import pallas as pl
+from jax.experimental.pallas import tpu as pltpu
 from jax.sharding import PartitionSpec as P
 
 EPSILON = 1e-06
+MESH = pl.DeviceIdType.MESH
+F32, BF16 = jnp.float32, jnp.bfloat16
+VM = pl.BlockSpec(memory_space=pltpu.VMEM)
+ANY = pl.BlockSpec(memory_space=pl.ANY)
+SM = pl.BlockSpec(memory_space=pltpu.SMEM)
+MIB = 2**20
+SEG = 8
+
+
+def nn(a, b):
+    return jnp.dot(a, b, preferred_element_type=F32)
+
+
+def nt(a, b):
+    return lax.dot_general(a, b, (((1,), (1,)), ((), ())), preferred_element_type=F32)
+
+
+def tn(a, b):
+    return lax.dot_general(a, b, (((0,), (0,)), ((), ())), preferred_element_type=F32)
+
+
+class Place:
+    def __init__(self):
+        me = lax.axis_index("dp")
+        self.me = me
+        self.core = core = lax.rem(me, 2)
+        x = lax.rem(lax.div(me, 2), 2)
+        y = lax.rem(lax.div(me, 4), 2)
+        self.z = z = lax.div(me, 8)
+        self.yx = yx = 2 * y + x
+        px, py = me + 2 - 4 * x, me + 4 - 8 * y
+        gx, gy = yx + 1 - 2 * x, yx + 2 - 4 * y
+        self.pa, self.pb = px + core * (py - px), py + core * (px - py)
+        self.ga, self.gb = gx + core * (gy - gx), gy + core * (gx - gy)
+        self.gd = 3 - yx
+        self.pc = me + 1 - 2 * core
+        self.other = 1 - core
+        self.zs = [lax.rem(z + d, 4) for d in (1, 2, 3)]
+        self.pz = [zz * 8 + lax.rem(me, 8) for zz in self.zs]
+
+
+def remote(src, dst, ssem, rsem, device):
+    return pltpu.make_async_remote_copy(
+        src_ref=src, dst_ref=dst, send_sem=ssem, recv_sem=rsem, device_id=(device,), device_id_type=MESH
+    )
+
+
+def entry_barrier(pl_, count, reach):
+    me = pl_.me
+    bar = pltpu.get_barrier_semaphore()
+    for p in [pl_.pc, pl_.pa, pl_.pb] + pl_.pz:
+        pl.semaphore_signal(bar, inc=1, device_id=(p,), device_id_type=MESH)
+    for d in range(1, reach + 1):
+
+        @pl.when(me >= d)
+        def _():
+            pl.semaphore_signal(bar, inc=1, device_id=(me - d,), device_id_type=MESH)
+
+        @pl.when(me + d < count)
+        def _():
+            pl.semaphore_signal(bar, inc=1, device_id=(me + d,), device_id_type=MESH)
+
+    pl.semaphore_wait(bar, 6 + jnp.minimum(me, reach) + jnp.minimum(count - 1 - me, reach))
+
+
+class Gather:
+    def __init__(self, p, buf, ssem, rsem):
+        self.p, self.buf, self.ssem, self.rsem = p, buf, ssem, rsem
+
+    def copy(self, slot):
+        p = self.p
+        if slot < 3:
+            src, dev = self.buf.at[p.core, p.yx, p.z], p.pz[slot]
+        else:
+            group = (p.yx, p.yx, p.ga, p.yx, p.ga, p.gb, p.gd)[slot - 3]
+            src, dev = self.buf.at[p.core, group], (p.pa, p.pb, p.pb, p.pc, p.pc, p.pc, p.pc)[slot - 3]
+        return remote(src, src, self.ssem.at[slot], self.rsem.at[slot], dev)
+
+    def start(self, *slots):
+        for s in slots:
+            self.copy(s).start()
+
+    def recv(self, *slots):
+        for s in slots:
+            self.copy(s).wait_recv()
+
+    def stage(self, n):
+        if n == 0:
+            self.start(0, 1, 2)
+        elif n == 1:
+            self.recv(0, 1, 2)
+            self.start(3, 4, 6)
+        elif n == 2:
+            self.recv(3)
+            self.start(5, 7)
+        elif n == 3:
+            self.recv(4)
+            self.start(8)
+            self.recv(5)
+            self.start(9)
+        else:
+            self.recv(6, 7, 8, 9)
+            for s in range(10):
+                self.copy(s).wait_send()
+
+
+def sequence_offset(lengths, first, rows):
+    t = first + lax.broadcasted_iota(jnp.int32, (rows, 128), 0)
+
+    def one(i, c):
+        bound, start = c
+        bound = bound + lengths[i]
+        return bound, jnp.where(t >= bound, bound, start)
+
+    _, start = lax.fori_loop(0, lengths.shape[0], one, (jnp.int32(0), jnp.zeros((rows, 128), jnp.int32)))
+    return t - start
+
+
+def one_minus_exp(v):
+    s = 1.0 + v * (1.0 / 8.0)
+    for k in (7.0, 6.0, 5.0, 4.0, 3.0, 2.0):
+        s = 1.0 + v * (1.0 / k) * s
+    return jnp.where(v > -0.5, -v * s, 1.0 - jnp.exp(v))
+
+
+def softplus(v):
+    return jnp.maximum(v, 0.0) + jnp.log1p(jnp.exp(-jnp.abs(v)))
+
+
+GELU_K = 0.7978845608028654
+
+
+def gelu_parts(v):
+    v2 = v * v
+    th = jnp.tanh(GELU_K * v * (1.0 + 0.044715 * v2))
+    half = 0.5 * (1.0 + th)
+    slope = half + 0.5 * v * (1.0 - th * th) * (GELU_K * (1.0 + 3.0 * 0.044715 * v2))
+    return v * half, slope
+
+
+def gelu(v):
+    return v * (0.5 * (1.0 + jnp.tanh(GELU_K * v * (1.0 + 0.044715 * (v * v)))))
+
+
+def flat(v):
+    return v.reshape(v.shape[0] * v.shape[1] * v.shape[2], v.shape[3])
+
+
+def chips(v):
+    return jnp.concatenate([v[yx, z] for z in range(4) for yx in range(4)], axis=0)
+
+
+def put_chips(part, half, v):
+    rows = v.shape[0] // 16
+    for z in range(4):
+        for yx in range(4):
+            part[half, yx, z] = v[(4 * z + yx) * rows : (4 * z + yx + 1) * rows]
+
+
+def put(page, v, row, group):
+    for i in range(v.shape[1] // 128):
+        page[group + i, row : row + v.shape[0], :] = v[:, i * 128 : (i + 1) * 128]
+
+
+def rows_loop(total, block, body):
+    def one(i, c):
+        body(pl.multiple_of(i * block, block))
+        return c
+
+    lax.fori_loop(0, total // block, one, 0)
+
+
+def blocks_loop(groups, total, block, body):
+    n = total // block
+
+    def one(i, c):
+        body(lax.div(i, n), pl.multiple_of(lax.rem(i, n) * block, block))
+        return c
+
+    lax.fori_loop(0, groups * n, one, 0)
+
+
+def pairs_loop(body):
+    def one(i, c):
+        body(2 * i, 0, False)
+        body(2 * i + 1, 1, i == 3)
+        return c
+
+    lax.fori_loop(0, 4, one, 0)
+
+
+def scan_segments(rows, factor, value, product, factor_row, value_row, product_row, reverse):
+    step = rows // SEG
+
+    def one(i, c):
+        j = step - 1 - i if reverse else i
+        out = []
+        for g in range(8):
+            h, q = c[g]
+            a = factor[g, pl.ds(factor_row + j, SEG, stride=step), :]
+            b = value[g, pl.ds(value_row + j, SEG, stride=step), :]
+            if reverse:
+                h = b + h
+                value[g, pl.ds(value_row + j, SEG, stride=step), :] = h
+                product[g, pl.ds(product_row + j, SEG, stride=step), :] = q
+                h, q = a * h, a * q
+            else:
+                h, q = a * h + b, a * q
+                value[g, pl.ds(value_row + j, SEG, stride=step), :] = h
+                product[g, pl.ds(product_row + j, SEG, stride=step), :] = q
+            out.append((h, q))
+        return tuple(out)
+
+    first = tuple((jnp.zeros((SEG, 128), F32), jnp.ones((SEG, 128), F32)) for _ in range(8))
+    return lax.fori_loop(0, step, one, first)
+
+
+def chain(ends, enter, reverse):
+    order = range(SEG - 1, -1, -1) if reverse else range(SEG)
+    inside, leave = [], []
+    for g in range(8):
+        h, q = ends[g]
+        v = enter[g]
+        rows = [None] * SEG
+        for s in order:
+            rows[s] = v
+            v = q[s : s + 1, :] * v + h[s : s + 1, :]
+        inside.append(jnp.concatenate(rows, axis=0))
+        leave.append(v)
+    return inside, leave
+
+
+def products(ends):
+    out = []
+    for g in range(8):
+        q = ends[g][1]
+        v = q[0:1, :]
+        for s in range(1, SEG):
+            v = v * q[s : s + 1, :]
+        out.append(v)
+    return out
+
+
+def carry_send(p, count, reach, sign, mine, inbox, ssem, rsem):
+    for d in range(1, reach + 1):
+
+        @pl.when((p.me + d < count) if sign > 0 else (p.me >= d))
+        def _(d=d):
+            remote(mine, inbox.at[d - 1], ssem.at[d - 1], rsem.at[d - 1], p.me + sign * d).start()
+
+
+def carry_wait(p, count, reach, sign, mine, inbox, ssem, rsem):
+    for d in range(1, reach + 1):
+        there = remote(mine, inbox.at[d - 1], ssem.at[d - 1], rsem.at[d - 1], p.me + sign * d)
+
+        @pl.when((p.me + d < count) if sign > 0 else (p.me >= d))
+        def _(there=there):
+            there.wait_send()
+
+        @pl.when((p.me >= d) if sign > 0 else (p.me + d < count))
+        def _(there=there):
+            there.wait_recv()
+
+
+def carry_fold(p, count, reach, sign, inbox):
+    v = [jnp.zeros((1, 128), F32) for _ in range(8)]
+    for d in range(reach, 0, -1):
+        for g in range(8):
+            v[g] = inbox[d - 1, 0, g : g + 1, :] * v[g] + inbox[d - 1, 1, g : g + 1, :]
+    return v
+
+
+def lanes(page, group, row, rows):
+    return jnp.concatenate([page[group, pl.ds(row, rows), :], page[group + 1, pl.ds(row, rows), :]], axis=1)
+
+
+def wide(page, groups, row, rows):
+    return jnp.concatenate([page[g, pl.ds(row, rows), :] for g in range(groups)], axis=1)
+
+
+def fold8(v):
+    return jnp.sum(v.reshape(v.shape[0] // 8, 8, v.shape[1]), axis=0)
+
+
+def forward_kernel(count, reach, *refs):
+    (tokens, cot, lengths, cw, cb, gb, dec, g1, g2, w_proj, w_out, w_gate, w_in, w_down,
+     out, o_par, o_gain, o_gg2, o_wproj, o_wgate, o_wout, o_gm, o_by, o_fac, o_gx, o_ga, o_sc, o_st, o_bx, o_coded,
+     o_mixed, o_u1, o_dmid, o_db,
+     wsmall, wproj, wgate, wout, wm, bx, by, fac, dr, pq, gx, ga, sc, ubuf, coded, mixed, middle, u2, hid, dgate, dup,
+     since, xh, ssmall, rsmall, sproj, rproj, sout, rout, sgate, rgate, smlp, rmlp, hin, mine, inbox,
+     gs, gr, ps, pr, hs, hr, cs, cr, osem) = refs
+    p = Place()
+    me = p.me
+    rows, width = tokens.shape
+    core0 = p.core == 0
+
+    xh[...] = jnp.zeros_like(xh)
+    inbox[...] = jnp.zeros_like(inbox)
+    entry_barrier(p, count, reach)
+
+    halo = remote(tokens.at[rows - 16 : rows], xh, hs.at[0], hr.at[0], me + 1)
+
+    @pl.when(me + 1 < count)
+    def _():
+        halo.start()
+
+    lane = lax.broadcasted_iota(jnp.int32, (32, 128), 1)
+    row = lax.broadcasted_iota(jnp.int32, (32, 128), 0)
+    spot = jnp.where(lane == lax.rem(me, 4) * 32 + row, 1.0, 0.0).astype(BF16)
+    gcol = lax.broadcasted_iota(jnp.int32, (24, width), 1)
+    grow = lax.broadcasted_iota(jnp.int32, (24, width), 0)
+    gspot = jnp.where(gcol == me * 24 + grow, 1.0, 0.0).astype(BF16)
+    ssmall[...] = jnp.zeros_like(ssmall)
+    ssmall[0:4, :] = nn(cw[...], spot)
+    ssmall[4:5, :] = nn(cb[...], spot)
+    ssmall[5:7, :] = nn(gb[...], spot)
+    ssmall[7:8, :] = nn(dec[...], spot)
+    r1, r2 = nn(g1[...], gspot), nn(g2[...], gspot)
+    for j in range(width // 128):
+        ssmall[8 + j : 9 + j, :] = r1[:, j * 128 : (j + 1) * 128]
+        ssmall[16 + j : 17 + j, :] = r2[:, j * 128 : (j + 1) * 128]
+    trades = [
+        remote(ssmall, rsmall, ps.at[0], pr.at[0], p.pc),
+        remote(sproj.at[p.other], rproj, ps.at[1], pr.at[1], p.pc),
+        remote(sgate.at[p.other], rgate, ps.at[2], pr.at[2], p.pc),
+        remote(sout.at[p.other], rout, ps.at[3], pr.at[3], p.pc),
+        remote(smlp.at[p.other], rmlp, ps.at[4], pr.at[4], p.pc),
+    ]
+    trades[0].start()
+    for h in range(2):
+        sproj[h] = w_proj[:, h * 1024 : (h + 1) * 1024].astype(F32)
+    trades[1].start()
+    for h in range(2):
+        sgate[h] = w_gate[:, h * 256 : (h + 1) * 256].astype(F32)
+        sout[h] = w_out[:, h * 512 : (h + 1) * 512].astype(F32)
+    trades[2].start()
+    trades[3].start()
+    smlp[0] = w_in[:, :1152].astype(F32)
+    smlp[1] = jnp.concatenate([w_in[:, 1152:], w_down[...]], axis=1).astype(F32)
+    trades[4].start()
+
+    chunks = [Gather(p, wsmall, gs.at[0], gr.at[0]), Gather(p, wproj, gs.at[1], gr.at[1]),
+              Gather(p, wgate, gs.at[2], gr.at[2]), Gather(p, wout, gs.at[3], gr.at[3])] + [
+        Gather(p, wm.at[k], gs.at[4 + k], gr.at[4 + k]) for k in range(3)
+    ]
+    batches = [chunks[0:2], chunks[2:4], chunks[4:5], chunks[5:6], chunks[6:7]]
+
+    def slab(mine_, theirs):
+        first = jnp.where(core0, mine_, theirs)
+        second = jnp.where(core0, theirs, mine_)
+        return jnp.concatenate([first, second], axis=0).astype(BF16)
+
+    trades[0].wait_recv()
+    both = ssmall[...] + rsmall[...]
+    wsmall[p.core, p.yx, p.z] = jnp.where(core0, both[0:16], both[16:32]).astype(BF16)
+    chunks[0].stage(0)
+    trades[1].wait_recv()
+    wproj[p.core, p.yx, p.z] = slab(sproj[p.core], rproj[...])
+    chunks[1].stage(0)
+    since[...] = sequence_offset(lengths, me * rows, rows)
+    trades[2].wait_recv()
+    wgate[p.core, p.yx, p.z] = slab(sgate[p.core], rgate[...])
+    trades[3].wait_recv()
+    wout[p.core, p.yx, p.z] = slab(sout[p.core], rout[...])
+    trades[4].wait_recv()
+    for k in range(3):
+        wm[k, p.core, p.yx, p.z] = slab(smlp[p.core, 24 * k : 24 * k + 24, :], rmlp[24 * k : 24 * k + 24, :])
+    for t in trades:
+        t.wait_send()
+
+    def slot(n):
+        for i, batch in enumerate(batches):
+            if 0 <= n - i <= 4 and not (i == 0 and n == 0):
+                for c in batch:
+                    c.stage(n - i)
+
+    outs = []
+
+    def save(src, dst):
+        c = pltpu.make_async_copy(src, dst, osem.at[len(outs)])
+        c.start()
+        outs.append(c)
+        return c
+
+    slot(1)
+    slot(2)
+    slot(3)
+    slot(4)
+
+    for g in range(8):
+        z_, yx_ = g // 2, 2 * (g % 2)
+        o_par[g] = wsmall[0, yx_, z_].astype(F32)[0:8] + wsmall[0, yx_ + 1, z_].astype(F32)[0:8]
+    gsum = [jnp.zeros((8, 128), F32), jnp.zeros((8, 128), F32)]
+    for z_ in range(4):
+        for yx_ in range(4):
+            gsum[0] = gsum[0] + wsmall[0, yx_, z_].astype(F32)[8:16]
+            gsum[1] = gsum[1] + wsmall[1, yx_, z_].astype(F32)[0:8]
+    o_gain[...] = jnp.zeros_like(o_gain)
+    for n in range(2):
+        for j in range(width // 128):
+            o_gain[n : n + 1, j * 128 : (j + 1) * 128] = gsum[n][j : j + 1]
+
+    @pl.when(me + 1 < count)
+    def _():
+        halo.wait_send()
+
+    @pl.when(me > 0)
+    def _():
+        halo.wait_recv()
+
+    def norm_rows(x, n):
+        inv = lax.rsqrt(jnp.mean(x * x, axis=1, keepdims=True) + EPSILON)
+        return (x * inv * o_gain[n : n + 1, :]).astype(BF16)
+
+    ubuf[0:16, :] = norm_rows(xh[...].astype(F32), 0)
+
+    def norm_one(r0):
+        ubuf[pl.ds(r0 + 16, 32), :] = norm_rows(tokens[pl.ds(r0, 32), :].astype(F32), 0)
+
+    rows_loop(rows, 32, norm_one)
+    save(ubuf.at[16 : rows + 16], o_u1)
+
+    def project(h, c):
+        cols = pl.ds(pl.multiple_of(h * 256, 256), 256)
+        v = nn(ubuf[...], chips(wproj[0, :, :, :, cols])).astype(BF16).astype(F32)
+        bx[2 * h], bx[2 * h + 1] = v[:, :128], v[:, 128:]
+        v = nn(ubuf[16:, :], chips(wproj[1, :, :, :, cols]))
+        by[2 * h], by[2 * h + 1] = v[:, :128], v[:, 128:]
+        return c
+
+    lax.fori_loop(0, 4, project, 0)
+    save(bx, o_bx)
+    save(by, o_by)
+    save(wproj, o_wproj)
+    slot(5)
+
+    def conv(g, r0):
+        par = o_par[g]
+        v = bx[g, pl.ds(r0 + 8, 72), :]
+        off = since[pl.ds(r0, 64), :]
+        total = par[4:5] + par[0:1] * v[8:72]
+        for k in range(1, 4):
+            total = total + par[k : k + 1] * jnp.where(off >= k, v[8 - k : 72 - k], 0.0)
+        coded[g, pl.ds(r0, 64), :] = total.astype(BF16)
+
+    blocks_loop(8, rows, 64, conv)
+    save(coded, o_coded)
+    save(wgate, o_wgate)
+
+    def gate_dots(h, c):
+        left = lanes(coded, 2 * h, 0, rows)
+        v = nn(left, wgate[0, :, h].reshape(256, 256))
+        gx[2 * h], gx[2 * h + 1] = v[:, :128], v[:, 128:]
+        v = nn(left, wgate[1, :, h].reshape(256, 256))
+        ga[2 * h], ga[2 * h + 1] = v[:, :128], v[:, 128:]
+        return c
+
+    lax.fori_loop(0, 4, gate_dots, 0)
+
+    def gates(g, r0):
+        par = o_par[g]
+        at = pl.ds(r0, 64)
+        fresh = since[at, :] == 0
+        gate_x = jax.nn.sigmoid(gx[g, at, :] + par[5:6])
+        gate_a = jax.nn.sigmoid(ga[g, at, :] + par[6:7])
+        log_a = -8.0 * gate_a * softplus(par[7:8])
+        factor = jnp.where(fresh, 0.0, jnp.exp(log_a))
+        scale = jnp.where(fresh, 1.0, jnp.sqrt(one_minus_exp(2.0 * log_a)))
+        gx[g, at, :] = gate_x
+        ga[g, at, :] = gate_a
+        fac[g, at, :] = factor
+        sc[g, at, :] = scale
+        dr[g, pl.ds(r0 + 8, 64), :] = scale * gate_x * coded[g, at, :].astype(F32)
+
+    blocks_loop(8, rows, 64, gates)
+    saved = [save(gx, o_gx), save(ga, o_ga), save(fac, o_fac), save(sc, o_sc)]
+
+    ends = scan_segments(rows, fac, dr, pq, 0, 8, 0, False)
+    _, leave = chain(ends, [jnp.zeros((1, 128), F32)] * 8, False)
+    whole = products(ends)
+    for g in range(8):
+        mine[0, g : g + 1, :] = whole[g]
+        mine[1, g : g + 1, :] = leave[g]
+    carry_send(p, count, reach, 1, mine, inbox, cs, cr)
+    slot(6)
+    carry_wait(p, count, reach, 1, mine, inbox, cs, cr)
+    enter = carry_fold(p, count, reach, 1, inbox)
+    inside, _ = chain(ends, enter, False)
+    for g in range(8):
+        hin[g] = inside[g]
+        dr[g, 0:8, :] = jnp.broadcast_to(enter[g], (8, 128))
+    step = rows // SEG
+
+    def states(g, c):
+        for s in range(SEG):
+            lo = s * step
+            st = dr[g, lo + 8 : lo + 8 + step, :] + pq[g, lo : lo + step, :] * hin[g, s : s + 1, :]
+            dr[g, lo + 8 : lo + 8 + step, :] = st
+            mixed[g, lo : lo + step, :] = (st * gelu(by[g, lo : lo + step, :])).astype(BF16)
+        return c
+
+    lax.fori_loop(0, 8, states, 0)
+    saved.append(save(dr, o_st))
+    save(mixed, o_mixed)
+    save(wout, o_wout)
+    middle[...] = nt(wide(mixed, 4, 0, rows), chips(wout[0])) + nt(
+        jnp.concatenate([mixed[g] for g in range(4, 8)], axis=1), chips(wout[1])
+    )
+
+    def norm_two(r0):
+        at = pl.ds(r0, 32)
+        m = middle[at, :] + tokens[at, :].astype(F32)
+        middle[at, :] = m
+        u2[at, :] = norm_rows(m, 1)
+
+    rows_loop(rows, 32, norm_two)
+    for c in saved:
+        c.wait()
+    fg, fu, fd, acc_out, acc_du = gx, ga, pq, sc, fac
+
+    for k in range(3):
+        if k > 0:
+            slot(6 + k)
+        w0 = flat(wm[k, 0])
+        w1 = flat(wm[k, 1])
+        wg, wu, wd = w0[:, :768], jnp.concatenate([w0[:, 768:], w1[:, :384]], axis=1), w1[:, 384:]
+        put(fg, nt(u2[...], wg), 0, 0)
+        put(fu, nt(u2[...], wu), 0, 0)
+        put(fd, nt(cot[...], wd), 0, 0)
+
+        def glu(r0):
+            at = pl.ds(r0, 32)
+            for g in range(6):
+                cols = slice(g * 128, (g + 1) * 128)
+                act, slope = gelu_parts(fg[g, at, :])
+                up, dh = fu[g, at, :], fd[g, at, :]
+                hid[at, cols] = (act * up).astype(BF16)
+                dgate[at, cols] = (dh * up * slope).astype(BF16)
+                dup[at, cols] = (dh * act).astype(BF16)
+
+        rows_loop(rows, 32, glu)
+        v = nn(hid[...], wd)
+        v2 = nn(dgate[...], wg) + nn(dup[...], wu)
+        for g in range(6):
+            cols = slice(g * 128, (g + 1) * 128)
+            if k == 0:
+                acc_out[g, 0:rows, :] = v[:, cols]
+                acc_du[g, 0:rows, :] = v2[:, cols]
+            else:
+                acc_out[g, 0:rows, :] += v[:, cols]
+                acc_du[g, 0:rows, :] += v2[:, cols]
+        gg = tn(dgate[...], u2[...]).astype(BF16)
+        gu = tn(dup[...], u2[...]).astype(BF16)
+        gd = tn(hid[...], cot[...]).astype(BF16)
+        wm[k, 0, :, :, :, 0:768] = gg.reshape(4, 4, 48, 768)
+        wm[k, 0, :, :, :, 768:1152] = gu[:, :384].reshape(4, 4, 48, 384)
+        wm[k, 1, :, :, :, 0:384] = gu[:, 384:].reshape(4, 4, 48, 384)
+        wm[k, 1, :, :, :, 384:1152] = gd.reshape(4, 4, 48, 768)
+        save(wm.at[k], o_gm.at[k])
+
+    o_gg2[...] = jnp.zeros_like(o_gg2)
+
+    def finish(r0):
+        at = pl.ds(r0, 32)
+        m, c = middle[at, :], cot[at, :].astype(F32)
+        out[at, :] = (m + wide(acc_out, 6, r0, 32)).astype(BF16)
+        du = wide(acc_du, 6, r0, 32)
+        inv = lax.rsqrt(jnp.mean(m * m, axis=1, keepdims=True) + EPSILON)
+        o_gg2[...] += fold8(du * m * inv)
+        gd_ = du * o_gain[1:2, :]
+        back = jnp.mean(gd_ * m, axis=1, keepdims=True)
+        dm = c + inv * gd_ - m * (inv * inv * inv * back)
+        hid[at, :] = dm.astype(BF16)
+        for g in range(6):
+            acc_out[g, at, :] = dm[:, g * 128 : (g + 1) * 128]
+
+    rows_loop(rows, 32, finish)
+    save(acc_out.at[0:6], o_dmid)
+    save(hid, o_db)
+    for c in outs:
+        if not any(c is s for s in saved):
+            c.wait()
+
+
+def forward_call(count, reach, args):
+    tokens = args[0]
+    rows, width = tokens.shape
+    S = jax.ShapeDtypeStruct
+    page = (8, rows, 128)
+    outs = [
+        (S((rows, width), BF16), VM),
+        (S((8, 8, 128), F32), VM),
+        (S((8, width), F32), VM),
+        (S((8, width), F32), VM),
+        (S((2, 4, 4, 48, 1024), BF16), ANY),
+        (S((2, 4, 4, 64, 256), BF16), ANY),
+        (S((2, 4, 4, 48, 512), BF16), ANY),
+        (S((3, 2, 4, 4, 48, 1152), BF16), ANY),
+        (S(page, F32), ANY),
+        (S(page, F32), ANY),
+        (S(page, F32), ANY),
+        (S(page, F32), ANY),
+        (S(page, F32), ANY),
+        (S((8, rows + 8, 128), F32), ANY),
+        (S((8, rows + 16, 128), F32), ANY),
+        (S(page, BF16), ANY),
+        (S(page, BF16), ANY),
+        (S((rows, width), BF16), ANY),
+        (S((6, rows, 128), F32), ANY),
+        (S((rows, width), BF16), ANY),
+    ]
+    V = pltpu.VMEM
+    dma = pltpu.SemaphoreType.DMA
+    scratch = [
+        V((2, 4, 4, 16, 128), BF16),
+        V((2, 4, 4, 48, 1024), BF16),
+        V((2, 4, 4, 64, 256), BF16),
+        V((2, 4, 4, 48, 512), BF16),
+        V((3, 2, 4, 4, 48, 1152), BF16),
+        V((8, rows + 16, 128), F32),
+        V(page, F32),
+        V(page, F32),
+        V((8, rows + 8, 128), F32),
+        V(page, F32),
+        V(page, F32),
+        V(page, F32),
+        V(page, F32),
+        V((rows + 16, width), BF16),
+        V(page, BF16),
+        V(page, BF16),
+        V((rows, width), F32),
+        V((rows, width), BF16),
+        V((rows, 768), BF16),
+        V((rows, 768), BF16),
+        V((rows, 768), BF16),
+        V((rows, 128), jnp.int32),
+        V((16, width), BF16),
+        V((32, 128), F32),
+        V((32, 128), F32),
+        V((2, 24, 1024), F32),
+        V((24, 1024), F32),
+        V((2, 24, 512), F32),
+        V((24, 512), F32),
+        V((2, 32, 256), F32),
+        V((32, 256), F32),
+        V((2, 72, 1152), F32),
+        V((72, 1152), F32),
+        V((8, 8, 128), F32),
+        V((2, 8, 128), F32),
+        V((reach, 2, 8, 128), F32),
+        dma((7, 10)),
+        dma((7, 10)),
+        dma((5,)),
+        dma((5,)),
+        dma((1,)),
+        dma((1,)),
+        dma((reach,)),
+        dma((reach,)),
+        dma((18,)),
+    ]
+    return pl.pallas_call(
+        functools.partial(forward_kernel, count, reach),
+        out_shape=[o[0] for o in outs],
+        in_specs=[VM, VM, SM] + [VM] * 11,
+        out_specs=[o[1] for o in outs],
+        scratch_shapes=scratch,
+        name="forward",
+        cost_estimate=pl.CostEstimate(flops=25 * 10**9, bytes_accessed=60 * 10**6, transcendentals=10**7),
+        compiler_params=pltpu.CompilerParams(
+            collective_id=0, has_side_effects=True, vmem_limit_bytes=62 * MIB
+        ),
+    )(*args)
+
+
+class Reduce:
+    def __init__(self, p, part, own, own_lead, bufs, lead, ssem, rsem, load=None):
+        self.p, self.part, self.load = p, part, load
+        self.whole, self.own_lead, self.bufs, self.lead = own, own_lead, bufs, lead
+        self.own = own.at[own_lead]
+        self.r0, self.ra, self.rb, self.rz, self.tot, self.rc = [b.at[lead] if lead else b for b in bufs]
+        self.ssem, self.rsem = ssem, rsem
+
+    def copy(self, slot):
+        p, own = self.p, self.own
+        src, dst, dev = (
+            (lambda: (self.part.at[p.other], self.r0, p.pc)),
+            (lambda: (own.at[p.gd], self.ra.at[1], p.pa)),
+            (lambda: (own.at[p.ga], self.ra.at[0], p.pa)),
+            (lambda: (own.at[p.gb], self.rb, p.pb)),
+            (lambda: (own.at[p.yx, p.zs[0]], self.rz.at[0], p.pz[0])),
+            (lambda: (own.at[p.yx, p.zs[1]], self.rz.at[1], p.pz[1])),
+            (lambda: (own.at[p.yx, p.zs[2]], self.rz.at[2], p.pz[2])),
+            (lambda: (self.tot.at[p.other], self.rc, p.pc)),
+        )[slot]()
+        return remote(src, dst, self.ssem.at[slot], self.rsem.at[slot], dev)
+
+    def add(self, group, which, *index):
+        buf = self.bufs[which]
+        for z in range(4):
+            at = self.own_lead + (group, z)
+            other = buf[self.lead + index + (z,)]
+            self.whole[at] = (self.whole[at].astype(F32) + other.astype(F32)).astype(BF16)
+
+    def stage(self, n):
+        p = self.p
+        if n == 0:
+            self.copy(0).start()
+            if self.load is not None:
+                self.load.start()
+        elif n == 1:
+            if self.load is not None:
+                self.load.wait()
+            self.copy(0).wait_recv()
+            for group, slot in ((p.gd, 1), (p.ga, 2)):
+                self.add(group, 0, group)
+                self.copy(slot).start()
+            for group in (p.gb, p.yx):
+                self.add(group, 0, group)
+        elif n == 2:
+            self.copy(1).wait_recv()
+            self.add(p.gb, 1, 1)
+            self.copy(3).start()
+            self.copy(2).wait_recv()
+            self.add(p.yx, 1, 0)
+        elif n == 3:
+            self.copy(3).wait_recv()
+            self.add(p.yx, 2)
+            for s in (4, 5, 6):
+                self.copy(s).start()
+        elif n == 4:
+            total = self.whole[self.own_lead + (p.yx, p.z)].astype(F32)
+            for d in range(3):
+                self.copy(4 + d).wait_recv()
+                total = total + self.bufs[3][self.lead + (d,)].astype(F32)
+            half = total.shape[0] // 2
+            self.bufs[4][self.lead + (0,)] = total[:half]
+            self.bufs[4][self.lead + (1,)] = total[half:]
+            self.copy(7).start()
+        else:
+            self.copy(7).wait_recv()
+            mine, theirs = self.bufs[4][self.lead + (p.core,)], self.bufs[5][self.lead + (...,)]
+            left = jnp.where(p.core == 0, mine, theirs)
+            right = jnp.where(p.core == 0, theirs, mine)
+            for s in range(8):
+                self.copy(s).wait_send()
+            return left, right
+
+
+class Totals:
+    def __init__(self, p, v, bufs, ssem, rsem):
+        self.p, self.v, self.bufs, self.ssem, self.rsem = p, v, bufs, ssem, rsem
+
+    def copy(self, slot):
+        p = self.p
+        dev = ([p.pc, p.pa, p.pb] + p.pz)[slot]
+        return remote(self.v.at[min(slot, 3)], self.bufs.at[slot], self.ssem.at[slot], self.rsem.at[slot], dev)
+
+    def stage(self, n):
+        if n < 3:
+            self.copy(n).start()
+        if n == 3:
+            for s in (3, 4, 5):
+                self.copy(s).start()
+
+    def step(self, n):
+        if n < 3:
+            self.copy(n).wait_recv()
+            self.v[n + 1] = self.v[n] + self.bufs[n]
+            return None
+        total = self.v[3]
+        for s in (3, 4, 5):
+            self.copy(s).wait_recv()
+            total = total + self.bufs[s]
+        for s in range(6):
+            self.copy(s).wait_send()
+        return total
+
+
+def backward_kernel(count, reach, *refs):
+    (tokens, lengths, par, gain, gg2, i_wproj, i_wgate, i_wout, i_gm, i_by, i_fac, i_gx, i_ga, i_sc, i_st, i_bx, i_coded,
+     i_mixed, i_u1, i_dmid, i_db,
+     grad_tokens, o_proj, o_out, o_gate, o_in, o_down, o_cw, o_cb, o_gb, o_dec, o_g1, o_g2,
+     wproj, wgate, wout, adj, fac, st, pp, gslot, coded, mixed, u1, db, dby, dgx, since,
+     own_m, gout, gpy, gpx, ggate,
+     m_r0, m_ra, m_rb, m_rz, m_tot, m_rc, p_r0, p_ra, p_rb, p_rz, p_tot, p_rc, t_r0, t_ra, t_rb, t_rz, t_tot, t_rc,
+     edge, sums, gsum, vsum, vbuf, hin, mine, inbox,
+     rs, rr, vs, vr, cs, cr, es, er, isem, gsem, lsem) = refs
+    p = Place()
+    me = p.me
+    rows, width = tokens.shape
+
+    inbox[...] = jnp.zeros_like(inbox)
+    edge[...] = jnp.zeros_like(edge)
+    entry_barrier(p, count, reach)
+
+    red_m = [
+        Reduce(p, i_gm.at[k], own_m, (k,), (m_r0, m_ra, m_rb, m_rz, m_tot, m_rc), (k,), rs.at[k], rr.at[k],
+               pltpu.make_async_copy(i_gm.at[k, p.core], own_m.at[k], lsem.at[k]))
+        for k in range(3)
+    ]
+    pbufs = (p_r0, p_ra, p_rb, p_rz, p_tot, p_rc)
+    red_out, red_py, red_px = [
+        Reduce(p, g, g, (p.core,), pbufs, (k,), rs.at[3 + k], rr.at[3 + k])
+        for k, g in enumerate((gout, gpy, gpx))
+    ]
+    red_gate = Reduce(p, ggate, ggate, (p.core,), (t_r0, t_ra, t_rb, t_rz, t_tot, t_rc), (), rs.at[6], rr.at[6])
+
+    for r in red_m:
+        r.stage(0)
+    loads = {}
+    for i, (name, src, dst) in enumerate((
+        ("db", i_db, db), ("wout", i_wout, wout), ("by", i_by, adj.at[:, 0:rows]), ("st", i_st, st), ("mixed", i_mixed, mixed),
+        ("u1", i_u1, u1), ("fac", i_fac, fac), ("coded", i_coded, coded), ("wgate", i_wgate, wgate),
+        ("wproj", i_wproj, wproj))):
+        loads[name] = pltpu.make_async_copy(src, dst, isem.at[i])
+        loads[name].start()
+
+    def fetch(g, slot):
+        return [
+            pltpu.make_async_copy(src.at[g], gslot.at[slot, i, 0:rows], gsem.at[slot, i])
+            for i, src in enumerate((i_gx, i_ga, i_sc))
+        ]
+
+    def fetch_bx(g, slot):
+        return pltpu.make_async_copy(i_bx.at[g], gslot.at[slot, 0], gsem.at[slot, 3])
+
+    for c in fetch(0, 0):
+        c.start()
+    since[...] = sequence_offset(lengths, me * rows, rows + 8)
+    sums[...] = jnp.zeros_like(sums)
+    gsum[...] = jnp.zeros_like(gsum)
+
+    loads["db"].wait()
+    loads["wout"].wait()
+
+    def mix_dots(h, c):
+        cols = pl.ds(pl.multiple_of(lax.rem(h, 2) * 256, 256), 256)
+        v = nn(db[...], chips(wout[lax.div(h, 2), :, :, :, cols]))
+        pp[2 * h], pp[2 * h + 1] = v[:, :128], v[:, 128:]
+        return c
+
+    lax.fori_loop(0, 4, mix_dots, 0)
+    loads["by"].wait()
+    loads["st"].wait()
+    red_m[0].stage(1)
+
+    def branch_y(g, r0):
+        at = pl.ds(r0, 64)
+        dm = pp[g, at, :]
+        act, slope = gelu_parts(adj[g, at, :])
+        adj[g, at, :] = dm * act
+        dby[g, at, :] = (dm * st[g, pl.ds(r0 + 8, 64), :] * slope).astype(BF16)
+
+    blocks_loop(8, rows, 64, branch_y)
+    red_m[1].stage(1)
+    loads["mixed"].wait()
+
+    def halves(target, left, page):
+        for h in range(2):
+            v = tn(left, jnp.concatenate([page[4 * h + i] for i in range(4)], axis=1))
+            put_chips(target, h, v.astype(BF16))
+
+    halves(gout, db[...], mixed)
+    red_out.stage(0)
+    red_m[2].stage(1)
+    loads["u1"].wait()
+    halves(gpy, u1[...], dby)
+    red_py.stage(0)
+    red_m[0].stage(2)
+    loads["fac"].wait()
+    ends = scan_segments(rows, fac, adj, pp, 0, 0, 0, True)
+    _, leave = chain(ends, [jnp.zeros((1, 128), F32)] * 8, True)
+    whole = products(ends)
+    for g in range(8):
+        mine[0, g : g + 1, :] = whole[g]
+        mine[1, g : g + 1, :] = leave[g]
+    carry_send(p, count, reach, -1, mine, inbox, cs, cr)
+    red_out.stage(1)
+    red_m[0].stage(3)
+    carry_wait(p, count, reach, -1, mine, inbox, cs, cr)
+    inside, _ = chain(ends, carry_fold(p, count, reach, -1, inbox), True)
+    for g in range(8):
+        hin[g] = inside[g]
+    step = rows // SEG
+
+    def adjoint(g, c):
+        for s in range(SEG):
+            lo = s * step
+            adj[g, lo : lo + step, :] += pp[g, lo : lo + step, :] * hin[g, s : s + 1, :]
+        return c
+
+    lax.fori_loop(0, 8, adjoint, 0)
+    red_m[1].stage(2)
+    red_py.stage(1)
+    loads["coded"].wait()
+    dga = mixed
+
+    def gate_back(g, slot, last):
+        @pl.when(jnp.logical_not(last))
+        def _():
+            for c_ in fetch(g + 1, 1 - slot):
+                c_.start()
+
+        for c_ in fetch(g, slot):
+            c_.wait()
+        row = par[g]
+        sp8 = -8.0 * softplus(row[7:8])
+
+        def block(i, acc):
+            r0 = pl.multiple_of(i * 64, 64)
+            at = pl.ds(r0, 64)
+            a, f = adj[g, at, :], fac[g, at, :]
+            gate_x, gate_a, scale = gslot[slot, 0, at, :], gslot[slot, 1, at, :], gslot[slot, 2, at, :]
+            code = coded[g, at, :].astype(F32)
+            before = st[g, pl.ds(r0, 72), :][7:71]
+            d_log = a * f * (before - gate_x * code * f / scale)
+            d_a = d_log * gate_a
+            d_ga = d_a * sp8 * (1.0 - gate_a)
+            d_part = a * scale * gate_x
+            d_gx = d_part * code * (1.0 - gate_x)
+            dgx[g, at, :] = d_gx.astype(BF16)
+            dga[g, at, :] = d_ga.astype(BF16)
+            adj[g, at, :] = d_part
+            return acc[0] + fold8(d_gx), acc[1] + fold8(d_ga), acc[2] + fold8(d_a)
+
+        zero = jnp.zeros((8, 128), F32)
+        acc = lax.fori_loop(0, rows // 64, block, (zero, zero, zero))
+        slope = jax.nn.sigmoid(row[7:8])
+        sums[g, 5:6, :] = jnp.sum(acc[0], axis=0, keepdims=True)
+        sums[g, 6:7, :] = jnp.sum(acc[1], axis=0, keepdims=True)
+        sums[g, 7:8, :] = jnp.sum(acc[2], axis=0, keepdims=True) * (-8.0 * slope)
+
+    pairs_loop(gate_back)
+    fetch_bx(0, 0).start()
+    load_dmid = pltpu.make_async_copy(i_dmid, st.at[0:6, 0:rows], isem.at[10])
+    load_dmid.start()
+    dbx = dgx
+    red_m[2].stage(2)
+    red_m[1].stage(3)
+    red_m[0].stage(4)
+    loads["wgate"].wait()
+
+    def gate_dots(h, c):
+        dx, da, code = lanes(dgx, 2 * h, 0, rows), lanes(dga, 2 * h, 0, rows), lanes(coded, 2 * h, 0, rows)
+        v = nt(dx, wgate[0, :, h].reshape(256, 256)) + nt(da, wgate[1, :, h].reshape(256, 256))
+        adj[2 * h, 0:rows, :] += v[:, :128]
+        adj[2 * h + 1, 0:rows, :] += v[:, 128:]
+        ggate[0, :, h] = tn(code, dx).astype(BF16).reshape(4, 64, 256)
+        ggate[1, :, h] = tn(code, da).astype(BF16).reshape(4, 64, 256)
+        return c
+
+    lax.fori_loop(0, 4, gate_dots, 0)
+    red_gate.stage(0)
+    edge[0] = adj[:, 0:8, :]
+    to_prev = remote(edge.at[0], edge.at[1], es.at[0], er.at[0], me - 1)
+
+    @pl.when(me > 0)
+    def _():
+        to_prev.start()
+
+    red_out.stage(2)
+    red_m[2].stage(3)
+    red_py.stage(2)
+    red_m[1].stage(4)
+
+    @pl.when(me > 0)
+    def _():
+        to_prev.wait_send()
+
+    @pl.when(me + 1 < count)
+    def _():
+        to_prev.wait_recv()
+
+    adj[:, rows : rows + 8, :] = edge[1]
+
+    def conv_back(g, slot, last):
+        @pl.when(jnp.logical_not(last))
+        def _():
+            fetch_bx(g + 1, 1 - slot).start()
+
+        fetch_bx(g, slot).wait()
+        row = par[g]
+
+        def block(i, acc):
+            r0 = pl.multiple_of(i * 64, 64)
+            d = adj[g, pl.ds(r0, 72), :]
+            off = since[pl.ds(r0, 72), :]
+            b = gslot[slot, 0, pl.ds(r0 + 8, 72), :]
+            own, off0 = d[0:64], off[0:64]
+            total = row[0:1] * own
+            out = [acc[0] + fold8(own * b[8:72])]
+            for k in range(1, 4):
+                total = total + row[k : k + 1] * jnp.where(off[k : 64 + k] >= k, d[k : 64 + k], 0.0)
+                out.append(acc[k] + fold8(own * jnp.where(off0 >= k, b[8 - k : 72 - k], 0.0)))
+            out.append(acc[4] + fold8(own))
+            dbx[g, pl.ds(r0, 64), :] = total.astype(BF16)
+            return tuple(out)
+
+        acc = lax.fori_loop(0, rows // 64, block, tuple(jnp.zeros((8, 128), F32) for _ in range(5)))
+        for k in range(5):
+            sums[g, k : k + 1, :] = jnp.sum(acc[k], axis=0, keepdims=True)
+
+    pairs_loop(conv_back)
+    halves(gpx, u1[...], dbx)
+    red_px.stage(0)
+    red_gate.stage(1)
+    red_out.stage(3)
+    red_py.stage(3)
+    red_m[2].stage(4)
+    loads["wproj"].wait()
+    du = nt(jnp.concatenate([dbx[g] for g in range(8)], axis=1), chips(wproj[0])) + nt(
+        jnp.concatenate([dby[g] for g in range(8)], axis=1), chips(wproj[1])
+    )
+    put(pp, du, 0, 0)
+    red_px.stage(1)
+    red_gate.stage(2)
+    red_out.stage(4)
+    red_py.stage(4)
+
+    load_dmid.wait()
+
+    def finish(r0):
+        at = pl.ds(r0, 32)
+        x = tokens[at, :].astype(F32)
+        d = wide(pp, 6, r0, 32)
+        inv = lax.rsqrt(jnp.mean(x * x, axis=1, keepdims=True) + EPSILON)
+        gsum[...] += fold8(d * x * inv)
+        scaled = d * gain[0:1, :]
+        back = jnp.mean(scaled * x, axis=1, keepdims=True)
+        grad_tokens[at, :] = (wide(st, 6, r0, 32) + inv * scaled - x * (inv * inv * inv * back)).astype(BF16)
+
+    rows_loop(rows, 32, finish)
+    vsum[0] = jnp.zeros((16, 1024), F32)
+    for g in range(8):
+        vsum[0, 0:8, g * 128 : (g + 1) * 128] = sums[g]
+    vsum[0, 8:9, 0:width] = jnp.sum(gsum[...], axis=0, keepdims=True)
+    vsum[0, 9:10, 0:width] = jnp.sum(gg2[...], axis=0, keepdims=True)
+    tot = Totals(p, vsum, vbuf, vs, vr)
+    tot.stage(0)
+    red_px.stage(2)
+    tot.step(0)
+    tot.stage(1)
+    red_gate.stage(3)
+    tot.step(1)
+    tot.stage(2)
+    red_px.stage(3)
+    tot.step(2)
+    tot.stage(3)
+    red_gate.stage(4)
+    for k in range(3):
+        left, right = red_m[k].stage(5)
+        lo = 24 * k
+        o_in[lo : lo + 24, 0:1152] = left
+        o_in[lo : lo + 24, 1152:1536] = right[:, :384]
+        o_down[lo : lo + 24, :] = right[:, 384:]
+    left, right = red_out.stage(5)
+    o_out[:, :512], o_out[:, 512:] = left, right
+    left, right = red_py.stage(5)
+    o_proj[:, 1024:1536], o_proj[:, 1536:2048] = left, right
+    red_px.stage(4)
+    left, right = red_gate.stage(5)
+    o_gate[:, :256], o_gate[:, 256:] = left, right
+    total = tot.step(3)
+    chan = pltpu.roll(total[0:8], lax.rem(1024 - 32 * me, 1024), 1)
+    o_cw[...] = chan[0:4, 0:32]
+    o_cb[...] = chan[4:5, 0:32]
+    o_gb[...] = chan[5:7, 0:32]
+    o_dec[...] = chan[7:8, 0:32]
+    gains = pltpu.roll(total[8:16], lax.rem(1024 - 24 * me, 1024), 1)
+    o_g1[...] = gains[0:1, 0:24]
+    o_g2[...] = gains[1:2, 0:24]
+    left, right = red_px.stage(5)
+    o_proj[:, 0:512], o_proj[:, 512:1024] = left, right
+
+
+def backward_call(count, reach, args):
+    tokens = args[0]
+    rows, width = tokens.shape
+    S = jax.ShapeDtypeStruct
+    V = pltpu.VMEM
+    dma = pltpu.SemaphoreType.DMA
+    page = (8, rows, 128)
+    outs = [
+        S((rows, width), BF16), S((24, 2048), F32), S((24, 1024), F32), S((32, 512), F32), S((72, 1536), F32),
+        S((72, 768), F32), S((4, 32), F32), S((1, 32), F32), S((2, 32), F32), S((1, 32), F32), S((1, 24), F32),
+        S((1, 24), F32),
+    ]
+
+    def bufs(n, r, c):
+        lead = (n,) if n else ()
+        return [V(lead + (4, 4, r, c), BF16), V(lead + (2, 4, r, c), BF16), V(lead + (4, r, c), BF16),
+                V(lead + (3, r, c), BF16), V(lead + (2, r // 2, c), F32), V(lead + (r // 2, c), F32)]
+
+    scratch = [
+        V((2, 4, 4, 48, 1024), BF16), V((2, 4, 4, 64, 256), BF16), V((2, 4, 4, 48, 512), BF16),
+        V((8, rows + 8, 128), F32),
+        V(page, F32),
+        V((8, rows + 8, 128), F32),
+        V(page, F32),
+        V((2, 3, rows + 16, 128), F32),
+        V(page, BF16), V(page, BF16), V((rows, width), BF16), V((rows, width), BF16),
+        V(page, BF16), V(page, BF16),
+        V((rows + 8, 128), jnp.int32),
+        V((3, 4, 4, 48, 1152), BF16),
+        V((2, 4, 4, 48, 512), BF16), V((2, 4, 4, 48, 512), BF16), V((2, 4, 4, 48, 512), BF16),
+        V((2, 4, 4, 64, 256), BF16),
+        *bufs(3, 48, 1152), *bufs(3, 48, 512), *bufs(0, 64, 256),
+        V((2, 8, 8, 128), F32),
+        V((8, 8, 128), F32), V((8, width), F32), V((4, 16, 1024), F32), V((6, 16, 1024), F32),
+        V((8, 8, 128), F32), V((2, 8, 128), F32), V((reach, 2, 8, 128), F32),
+        dma((7, 8)), dma((7, 8)), dma((6,)), dma((6,)), dma((reach,)), dma((reach,)), dma((1,)), dma((1,)),
+        dma((11,)), dma((2, 4)), dma((3,)),
+    ]
+    return pl.pallas_call(
+        functools.partial(backward_kernel, count, reach),
+        out_shape=outs,
+        in_specs=[VM, SM, VM, VM, VM] + [ANY] * 16,
+        out_specs=[VM] * len(outs),
+        scratch_shapes=scratch,
+        name="backward",
+        cost_estimate=pl.CostEstimate(flops=12 * 10**9, bytes_accessed=60 * 10**6, transcendentals=10**7),
+        compiler_params=pltpu.CompilerParams(
+            collective_id=1, has_side_effects=True, vmem_limit_bytes=63 * MIB
+        ),
+    )(*args)
 
 
 def from_behind(x, axis, by):
@@ -135,7 +1262,7 @@
     blocks_w = w_gates.reshape(head_count, block_size, 2 * block_size)
     coded_heads = coded_rows.reshape(tok_rows, head_count, block_size)
     gate_pre = jnp.einsum("thi,hij->thj", coded_heads, blocks_w, preferred_element_type=jnp.float32)
-    gate_fn = partial(gate_math, fresh_row=fresh_row)
+    gate_fn = functools.partial(gate_math, fresh_row=fresh_row)
     (factor, drive_term), gate_back = jax.vjp(
         gate_fn, gate_pre, b_gates, w_decay, coded_rows.astype(jnp.float32)
     )
@@ -271,6 +1398,32 @@
     )
 
 
+def kernels_step(
+    tokens, cotangent, lengths, gain_norm1, gain_norm2, proj_in, out_proj, gate_blocks, conv_weight, conv_bias, gate_bias,
+    decay_param, mlp_in, mlp_down,
+):
+    count = lax.axis_size("dp")
+    rows = tokens.shape[0]
+    longest = rows * count // 12
+    reach = -(-(longest - 1) // rows)
+    (output, par, gain, gg2, wproj, wgate, wout, gm, by, fac, gx, ga, sc, st, bx, coded, mixed, u1, dmid, db) = forward_call(
+        count, reach,
+        (tokens, cotangent, lengths, conv_weight, conv_bias[None], gate_bias, decay_param[None], gain_norm1[None],
+         gain_norm2[None], proj_in, out_proj, gate_blocks, mlp_in, mlp_down),
+    )
+    (grad_tokens, g_proj, g_out, g_gate, g_in, g_down, g_cw, g_cb, g_gb, g_dec, g_n1, g_n2) = backward_call(
+        count, reach,
+        (tokens, lengths, par, gain, gg2, wproj, wgate, wout, gm, by, fac, gx, ga, sc, st, bx, coded, mixed, u1, dmid, db),
+    )
+    return (
+        output, grad_tokens, g_n1[0], g_n2[0], g_proj, g_out, g_gate, g_cw, g_cb[0], g_gb, g_dec[0], g_in, g_down,
+    )
+
+
+def fits(mesh):
+    return mesh.shape["dp"] == 32
+
+
 def solution(mesh):
     placed = (
         P("dp", None),
@@ -289,7 +1442,7 @@
         P("dp", None),
     )
     return jax.shard_map(
-        per_device,
+        kernels_step if fits(mesh) else per_device,
         mesh=mesh,
         in_specs=placed,
         out_specs=(

time: 1990 us -> 269 us (0.14)
  local copies, waits for them, and re-layouts: 681 us -> 10.1 us
  waiting for transfers between devices: 642 us -> 0 us
  blocking collectives: 310 us -> 0 us
  Pallas kernels: 0 us -> 252 us
  other arithmetic: 213 us -> 0 us
  matrix products: 98.7 us -> 0 us
    slice x143 -> x0, local copies, waits for them, and re-layouts: 380 us -> none  [the longest x69 227 us: per_device(): lax.associative_scan(combine_steps, (ahead_factor, d_state), reverse=True...]
    unnamed x13 -> x0, waiting for transfers between devices: 370 us -> none
    reduce_scatter x2 -> x0, waiting for transfers between devices: 271 us -> none  [the longest x1 136 us: per_device(): lax.psum_scatter(jnp.concatenate([part_proj, part_out], axis=1), 'dp', sc...]
    pallas_call x0 -> x2, Pallas kernels: none -> 252 us  [the longest x1 130 us: forward_call(): pl.pallas_call(functools.partial(forward_kernel, count, reach), out_shape...]
    all_gather x6 -> x0, blocking collectives: 229 us -> none  [the longest x4 152 us: prefix(): gathered = jax.tree.map(lambda a: lax.all_gather(a, axis), part)]
    pad x68 -> x0, local copies, waits for them, and re-layouts: 178 us -> none  [the longest x34 91.9 us: per_device(): lax.associative_scan(combine_steps, (factor, drive_term), axis=0)]
    dot_general x18 -> x0, matrix products: 98.7 us -> none  [the longest x1 12.9 us: per_device(): jnp.einsum('td,fd->tf', u_two, w_mlp[:, :model_width], preferred_element_...]
    add x84 -> x0, other arithmetic: 85.3 us -> none  [the longest x48 32.6 us: combine_steps(): return (earlier[0] * later[0], later[0] * earlier[1] + later[1])]
  transfers between devices with their start and end apart: 12 -> 0, of which waited for: 5 -> 0; matrix products, arithmetic and copies ran while one was open for 26% -> 0% of each run, Pallas kernels for 0% -> 0%
where the time goes in v1:
time: 269 us; the launch traced here: 264 us
  Pallas kernels  252 us (94%)
  local copies, waits for them, and re-layouts  10.1 us (4%)
    pallas_call x1, Pallas kernels, forward_call(): pl.pallas_call(functools.partial(forward_kernel, count, reach), out_shape...  130 us
    pallas_call x1, Pallas kernels, backward_call(): pl.pallas_call(functools.partial(backward_kernel, count, reach), out_shap...  122 us
    unnamed x37, local copies, waits for them, and re-layouts  10.1 us

profile of v1, /device:TPU:0, one launch (start us, length us, event | category | flops | bytes accessed | tf_op | source)
XLA Modules:
  0.0 263.8 jit_solution(17090594368828053036)
XLA Ops:
  0.6 130.2 %forward.1 = (bf16[768,768]{1,0:T(8,128)(2,1)}, f32[8,8,128]{2,1,0:T(8,128)}, f32[8,768]{1,0:T(8,128)}, f32[8,768]{1,0:T(8,128)}, bf16[2,4,4,48,1024]{4,3,2,1,0:...) custom-call(bf16[768,768]{1,0:T(8,128)(2,1)} %refs_0_.3, ...), custom_call_target="tpu_custom_call" | custom-call | flops 24999999488 | bytes 60000000 | tf_op jit(solution)/shard_map/forward/pallas_call | solution.py:671
  130.9 122.3 %backward.1 = (bf16[768,768]{1,0:T(8,128)(2,1)}, f32[24,2048]{1,0:T(8,128)}, f32[24,1024]{1,0:T(8,128)}, f32[32,512]{1,0:T(8,128)}, f32[72,1536]{1,0:T(8,128)}, ...) custom-call(bf16[768,768]{1,0:T(8,128)(2,1)} %refs_0_.3, ...), custom_call_target="tpu_custom_call" | custom-call | flops 12000000000 | bytes 60000000 | tf_op jit(solution)/shard_map/backward/pallas_call | solution.py:1124
  253.2 0.0 copy-start
  253.2 2.5 copy.40
  255.6 0.0 copy-done
  255.6 0.0 copy-start.11
  255.6 0.0 copy-start.10
  255.6 0.0 copy-start.3
  255.6 0.0 copy-start.4
  255.7 0.0 copy-start.5
  255.7 0.0 copy-start.6
  255.7 0.0 copy-start.9
  255.7 0.0 copy-start.7
  255.7 0.0 copy-start.8
  255.7 0.0 copy-start.1
  255.7 0.0 copy-start.2
  255.7 1.0 copy.41
  256.7 0.0 copy-done.11
  256.7 0.5 copy.42
  257.3 0.0 copy-done.10
  257.3 0.5 copy.43
  257.8 0.0 copy-done.3
  257.8 0.7 copy.44
  258.4 0.0 copy-done.4
  258.4 0.6 copy.45
  259.1 0.0 copy-done.5
  259.1 0.6 copy.46
  259.7 0.0 copy-done.6
  259.7 0.6 copy.47
  260.3 0.0 copy-done.9
  260.3 0.5 copy.48
  260.8 0.0 copy-done.7
  260.8 0.6 copy.49
  261.4 0.0 copy-done.8
  261.4 0.5 copy.50
  261.9 0.0 copy-done.1
  261.9 0.8 copy.51
  262.7 0.0 copy-done.2
  262.7 0.7 copy.52
Async XLA Ops:
  253.2 2.5 copy-start
  255.6 1.1 copy-start.11
  255.6 1.6 copy-start.10
  255.6 2.1 copy-start.3
  255.6 2.8 %copy-start.4 = (f32[24,1024]{1,0:T(8,128)S(1)}, f32[24,1024]{1,0:T(8,128)}, u32[]{:S(2)}) copy-start(f32[24,1024]{1,0:T(8,128)} %get-tuple-element.95) | copy-start | bytes 294916
  255.7 3.4 %copy-start.5 = (f32[32,512]{1,0:T(8,128)S(1)}, f32[32,512]{1,0:T(8,128)}, u32[]{:S(2)}) copy-start(f32[32,512]{1,0:T(8,128)} %get-tuple-element.96) | copy-start | bytes 196612
  255.7 4.1 %copy-start.6 = (f32[4,32]{1,0:T(4,128)S(1)}, f32[4,32]{1,0:T(4,128)}, u32[]{:S(2)}) copy-start(f32[4,32]{1,0:T(4,128)} %get-tuple-element.97) | copy-start | bytes 1540
  255.7 4.6 %copy-start.9 = (f32[1,32]{1,0:T(1,128)S(1)}, f32[1,32]{1,0:T(1,128)}, u32[]{:S(2)}) copy-start(f32[1,32]{1,0:T(1,128)} %get-tuple-element.72) | copy-start | bytes 388
  255.7 5.1 %copy-start.7 = (f32[2,32]{1,0:T(2,128)S(1)}, f32[2,32]{1,0:T(2,128)}, u32[]{:S(2)}) copy-start(f32[2,32]{1,0:T(2,128)} %get-tuple-element.99) | copy-start | bytes 772
  255.7 5.7 %copy-start.8 = (f32[1,32]{1,0:T(1,128)S(1)}, f32[1,32]{1,0:T(1,128)}, u32[]{:S(2)}) copy-start(f32[1,32]{1,0:T(1,128)} %get-tuple-element.74) | copy-start | bytes 388
  255.7 6.2 %copy-start.1 = (f32[72,1536]{1,0:T(8,128)S(1)}, f32[72,1536]{1,0:T(8,128)}, u32[]{:S(2)}) copy-start(f32[72,1536]{1,0:T(8,128)} %get-tuple-element.101) | copy-start | bytes 1327108
  255.7 7.0 %copy-start.2 = (f32[72,768]{1,0:T(8,128)S(1)}, f32[72,768]{1,0:T(8,128)}, u32[]{:S(2)}) copy-start(f32[72,768]{1,0:T(8,128)} %get-tuple-element.102) | copy-start | bytes 663556

commit v2 on v1

--- a/solution.py
+++ b/solution.py
@@ -15,6 +15,8 @@
 SM = pl.BlockSpec(memory_space=pltpu.SMEM)
 MIB = 2**20
 SEG = 8
+STEP = 97
+PAD = 8
 
 
 def nn(a, b):
@@ -126,11 +128,13 @@
     return t - start
 
 
-def one_minus_exp(v):
-    s = 1.0 + v * (1.0 / 8.0)
-    for k in (7.0, 6.0, 5.0, 4.0, 3.0, 2.0):
-        s = 1.0 + v * (1.0 / k) * s
-    return jnp.where(v > -0.5, -v * s, 1.0 - jnp.exp(v))
+def one_minus_square(v, root):
+    series = 1.0 / 2.0 + v * (1.0 / 6.0 + v * (1.0 / 24.0 + v * (1.0 / 120.0 + v * (1.0 / 720.0))))
+    return jnp.where(v > -0.125, -v - v * v * series, 1.0 - root * root)
+
+
+def root_of(v):
+    return v * lax.rsqrt(jnp.maximum(v, 1e-37))
 
 
 def softplus(v):
@@ -160,6 +164,10 @@
     return jnp.concatenate([v[yx, z] for z in range(4) for yx in range(4)], axis=0)
 
 
+def whole_w(w):
+    return jnp.concatenate([chips(w[0]), chips(w[1])], axis=1)
+
+
 def put_chips(part, half, v):
     rows = v.shape[0] // 16
     for z in range(4):
@@ -199,30 +207,37 @@
     lax.fori_loop(0, 4, one, 0)
 
 
-def scan_segments(rows, factor, value, product, factor_row, value_row, product_row, reverse):
-    step = rows // SEG
-
+def scan_segments(factor, value, product, factor_row, value_row, product_row, reverse):
     def one(i, c):
-        j = step - 1 - i if reverse else i
+        j = STEP - 1 - i if reverse else i
         out = []
         for g in range(8):
             h, q = c[g]
-            a = factor[g, pl.ds(factor_row + j, SEG, stride=step), :]
-            b = value[g, pl.ds(value_row + j, SEG, stride=step), :]
+            a = factor[g, pl.ds(factor_row + j, SEG, stride=STEP), :]
+            b = value[g, pl.ds(value_row + j, SEG, stride=STEP), :]
             if reverse:
                 h = b + h
-                value[g, pl.ds(value_row + j, SEG, stride=step), :] = h
-                product[g, pl.ds(product_row + j, SEG, stride=step), :] = q
+                value[g, pl.ds(value_row + j, SEG, stride=STEP), :] = h
+                product[g, pl.ds(product_row + j, SEG, stride=STEP), :] = q
                 h, q = a * h, a * q
             else:
                 h, q = a * h + b, a * q
-                value[g, pl.ds(value_row + j, SEG, stride=step), :] = h
-                product[g, pl.ds(product_row + j, SEG, stride=step), :] = q
+                value[g, pl.ds(value_row + j, SEG, stride=STEP), :] = h
+                product[g, pl.ds(product_row + j, SEG, stride=STEP), :] = q
             out.append((h, q))
         return tuple(out)
 
     first = tuple((jnp.zeros((SEG, 128), F32), jnp.ones((SEG, 128), F32)) for _ in range(8))
-    return lax.fori_loop(0, step, one, first)
+    return lax.fori_loop(0, STEP, one, first)
+
+
+def segment_rows(inside, i, block):
+    rest = inside[i : i + 1, :]
+    first = jnp.broadcast_to(rest, (8, 128))
+    if i:
+        spot = lax.broadcasted_iota(jnp.int32, (8, 128), 0)
+        first = jnp.where(spot < i, inside[i - 1 : i, :], first)
+    return jnp.concatenate([first, jnp.broadcast_to(rest, (block - 8, 128))], axis=0)
 
 
 def chain(ends, enter, reverse):
@@ -294,11 +309,11 @@
 
 def forward_kernel(count, reach, *refs):
     (tokens, cot, lengths, cw, cb, gb, dec, g1, g2, w_proj, w_out, w_gate, w_in, w_down,
-     out, o_par, o_gain, o_gg2, o_wproj, o_wgate, o_wout, o_gm, o_by, o_fac, o_gx, o_ga, o_sc, o_st, o_bx, o_coded,
-     o_mixed, o_u1, o_dmid, o_db,
-     wsmall, wproj, wgate, wout, wm, bx, by, fac, dr, pq, gx, ga, sc, ubuf, coded, mixed, middle, u2, hid, dgate, dup,
-     since, xh, ssmall, rsmall, sproj, rproj, sout, rout, sgate, rgate, smlp, rmlp, hin, mine, inbox,
-     gs, gr, ps, pr, hs, hr, cs, cr, osem) = refs
+     out, o_par, o_gain, o_gg2, o_wbx, o_wby, o_wgate, o_wout, o_by, o_fac, o_gx, o_ga, o_sc, o_st, o_bx, o_coded,
+     o_mixed, o_u1, o_dmid, o_db, o_part0, o_part1, o_part2,
+     wsmall, wbx, wby, wgate, wout, wm, bx, by, fac, dr, pq, gx, ga, sc, ubuf, coded, mixed, dup,
+     since, rate, xh, ssmall, rsmall, sproj, rproj, sout, rout, sgate, rgate, smlp, rmlp, hin, mine, inbox, m_r0, m_ra, m_rb,
+     gs, gr, ps, pr, hs, hr, cs, cr, rs, rr, osem, free) = refs
     p = Place()
     me = p.me
     rows, width = tokens.shape
@@ -306,6 +321,8 @@
 
     xh[...] = jnp.zeros_like(xh)
     inbox[...] = jnp.zeros_like(inbox)
+    fac[:, rows:, :] = jnp.ones((8, PAD, 128), F32)
+    dr[:, rows + 8 :, :] = jnp.zeros((8, PAD, 128), F32)
     entry_barrier(p, count, reach)
 
     halo = remote(tokens.at[rows - 16 : rows], xh, hs.at[0], hr.at[0], me + 1)
@@ -331,29 +348,33 @@
         ssmall[16 + j : 17 + j, :] = r2[:, j * 128 : (j + 1) * 128]
     trades = [
         remote(ssmall, rsmall, ps.at[0], pr.at[0], p.pc),
-        remote(sproj.at[p.other], rproj, ps.at[1], pr.at[1], p.pc),
+        remote(sproj.at[0, p.other], rproj.at[0], ps.at[1], pr.at[1], p.pc),
         remote(sgate.at[p.other], rgate, ps.at[2], pr.at[2], p.pc),
-        remote(sout.at[p.other], rout, ps.at[3], pr.at[3], p.pc),
-        remote(smlp.at[p.other], rmlp, ps.at[4], pr.at[4], p.pc),
+        remote(sproj.at[1, p.other], rproj.at[1], ps.at[3], pr.at[3], p.pc),
+        remote(sout.at[p.other], rout, ps.at[4], pr.at[4], p.pc),
+        remote(smlp.at[p.other], rmlp, ps.at[5], pr.at[5], p.pc),
     ]
     trades[0].start()
-    for h in range(2):
-        sproj[h] = w_proj[:, h * 1024 : (h + 1) * 1024].astype(F32)
-    trades[1].start()
+    for n in range(2):
+        for h in range(2):
+            lo = n * 1024 + h * 512
+            sproj[n, h] = w_proj[:, lo : lo + 512].astype(F32)
+        if n == 0:
+            trades[1].start()
     for h in range(2):
         sgate[h] = w_gate[:, h * 256 : (h + 1) * 256].astype(F32)
         sout[h] = w_out[:, h * 512 : (h + 1) * 512].astype(F32)
     trades[2].start()
     trades[3].start()
+    trades[4].start()
     smlp[0] = w_in[:, :1152].astype(F32)
     smlp[1] = jnp.concatenate([w_in[:, 1152:], w_down[...]], axis=1).astype(F32)
-    trades[4].start()
-
-    chunks = [Gather(p, wsmall, gs.at[0], gr.at[0]), Gather(p, wproj, gs.at[1], gr.at[1]),
-              Gather(p, wgate, gs.at[2], gr.at[2]), Gather(p, wout, gs.at[3], gr.at[3])] + [
-        Gather(p, wm.at[k], gs.at[4 + k], gr.at[4 + k]) for k in range(3)
+    trades[5].start()
+
+    g_small, g_bx, g_gate, g_by, g_out = [
+        Gather(p, w, gs.at[i], gr.at[i]) for i, w in enumerate((wsmall, wbx, wgate, wby, wout))
     ]
-    batches = [chunks[0:2], chunks[2:4], chunks[4:5], chunks[5:6], chunks[6:7]]
+    g_m = [Gather(p, wm.at[k], gs.at[5 + k], gr.at[5 + k]) for k in range(3)]
 
     def slab(mine_, theirs):
         first = jnp.where(core0, mine_, theirs)
@@ -363,26 +384,19 @@
     trades[0].wait_recv()
     both = ssmall[...] + rsmall[...]
     wsmall[p.core, p.yx, p.z] = jnp.where(core0, both[0:16], both[16:32]).astype(BF16)
-    chunks[0].stage(0)
+    g_small.stage(0)
     trades[1].wait_recv()
-    wproj[p.core, p.yx, p.z] = slab(sproj[p.core], rproj[...])
-    chunks[1].stage(0)
-    since[...] = sequence_offset(lengths, me * rows, rows)
+    wbx[p.core, p.yx, p.z] = slab(sproj[0, p.core], rproj[0])
+    g_bx.stage(0)
     trades[2].wait_recv()
     wgate[p.core, p.yx, p.z] = slab(sgate[p.core], rgate[...])
     trades[3].wait_recv()
+    wby[p.core, p.yx, p.z] = slab(sproj[1, p.core], rproj[1])
+    trades[4].wait_recv()
     wout[p.core, p.yx, p.z] = slab(sout[p.core], rout[...])
-    trades[4].wait_recv()
+    trades[5].wait_recv()
     for k in range(3):
         wm[k, p.core, p.yx, p.z] = slab(smlp[p.core, 24 * k : 24 * k + 24, :], rmlp[24 * k : 24 * k + 24, :])
-    for t in trades:
-        t.wait_send()
-
-    def slot(n):
-        for i, batch in enumerate(batches):
-            if 0 <= n - i <= 4 and not (i == 0 and n == 0):
-                for c in batch:
-                    c.stage(n - i)
 
     outs = []
 
@@ -392,14 +406,23 @@
         outs.append(c)
         return c
 
-    slot(1)
-    slot(2)
-    slot(3)
-    slot(4)
+    g_small.stage(1)
+    g_bx.stage(1)
+    g_gate.stage(0)
+    since[...] = sequence_offset(lengths, me * rows, rows)
+    for t in trades:
+        t.wait_send()
+    g_small.stage(2)
+    g_bx.stage(2)
+    g_gate.stage(1)
+    g_by.stage(0)
+    g_small.stage(3)
+    g_small.stage(4)
 
     for g in range(8):
         z_, yx_ = g // 2, 2 * (g % 2)
         o_par[g] = wsmall[0, yx_, z_].astype(F32)[0:8] + wsmall[0, yx_ + 1, z_].astype(F32)[0:8]
+        rate[g] = -8.0 * softplus(o_par[g])
     gsum = [jnp.zeros((8, 128), F32), jnp.zeros((8, 128), F32)]
     for z_ in range(4):
         for yx_ in range(4):
@@ -428,21 +451,32 @@
         ubuf[pl.ds(r0 + 16, 32), :] = norm_rows(tokens[pl.ds(r0, 32), :].astype(F32), 0)
 
     rows_loop(rows, 32, norm_one)
-    save(ubuf.at[16 : rows + 16], o_u1)
-
-    def project(h, c):
-        cols = pl.ds(pl.multiple_of(h * 256, 256), 256)
-        v = nn(ubuf[...], chips(wproj[0, :, :, :, cols])).astype(BF16).astype(F32)
+    saved_u1 = save(ubuf.at[16 : rows + 16], o_u1)
+    g_bx.stage(3)
+    g_gate.stage(2)
+    g_by.stage(1)
+    g_out.stage(0)
+    g_bx.stage(4)
+
+    def project_x(h, c):
+        cols = pl.ds(pl.multiple_of(lax.rem(h, 2) * 256, 256), 256)
+        v = nn(ubuf[...], chips(wbx[lax.div(h, 2), :, :, :, cols])).astype(BF16).astype(F32)
         bx[2 * h], bx[2 * h + 1] = v[:, :128], v[:, 128:]
-        v = nn(ubuf[16:, :], chips(wproj[1, :, :, :, cols]))
+        return c
+
+    def project_y(h, c):
+        cols = pl.ds(pl.multiple_of(lax.rem(h, 2) * 256, 256), 256)
+        v = nn(ubuf[16:, :], chips(wby[lax.div(h, 2), :, :, :, cols]))
         by[2 * h], by[2 * h + 1] = v[:, :128], v[:, 128:]
         return c
 
-    lax.fori_loop(0, 4, project, 0)
-    save(bx, o_bx)
-    save(by, o_by)
-    save(wproj, o_wproj)
-    slot(5)
+    lax.fori_loop(0, 4, project_x, 0)
+    saved_bx = save(bx, o_bx)
+    save(wbx, o_wbx)
+    g_gate.stage(3)
+    g_by.stage(2)
+    g_out.stage(1)
+    g_m[0].stage(0)
 
     def conv(g, r0):
         par = o_par[g]
@@ -454,7 +488,8 @@
         coded[g, pl.ds(r0, 64), :] = total.astype(BF16)
 
     blocks_loop(8, rows, 64, conv)
-    save(coded, o_coded)
+    saved_c = save(coded, o_coded)
+    g_gate.stage(4)
     save(wgate, o_wgate)
 
     def gate_dots(h, c):
@@ -467,15 +502,21 @@
 
     lax.fori_loop(0, 4, gate_dots, 0)
 
+    g_by.stage(3)
+    g_out.stage(2)
+    g_m[0].stage(1)
+    g_m[1].stage(0)
+
     def gates(g, r0):
         par = o_par[g]
         at = pl.ds(r0, 64)
         fresh = since[at, :] == 0
         gate_x = jax.nn.sigmoid(gx[g, at, :] + par[5:6])
         gate_a = jax.nn.sigmoid(ga[g, at, :] + par[6:7])
-        log_a = -8.0 * gate_a * softplus(par[7:8])
-        factor = jnp.where(fresh, 0.0, jnp.exp(log_a))
-        scale = jnp.where(fresh, 1.0, jnp.sqrt(one_minus_exp(2.0 * log_a)))
+        log_a = gate_a * rate[g, 7:8, :]
+        decay = jnp.exp(log_a)
+        factor = jnp.where(fresh, 0.0, decay)
+        scale = jnp.where(fresh, 1.0, root_of(one_minus_square(2.0 * log_a, decay)))
         gx[g, at, :] = gate_x
         ga[g, at, :] = gate_a
         fac[g, at, :] = factor
@@ -483,16 +524,24 @@
         dr[g, pl.ds(r0 + 8, 64), :] = scale * gate_x * coded[g, at, :].astype(F32)
 
     blocks_loop(8, rows, 64, gates)
-    saved = [save(gx, o_gx), save(ga, o_ga), save(fac, o_fac), save(sc, o_sc)]
-
-    ends = scan_segments(rows, fac, dr, pq, 0, 8, 0, False)
+    saved = [save(gx, o_gx), save(ga, o_ga), save(fac.at[:, 0:rows], o_fac), save(sc, o_sc)]
+
+    g_by.stage(4)
+    g_out.stage(3)
+    g_m[0].stage(2)
+    ends = scan_segments(fac, dr, pq, 0, 8, 0, False)
     _, leave = chain(ends, [jnp.zeros((1, 128), F32)] * 8, False)
     whole = products(ends)
     for g in range(8):
         mine[0, g : g + 1, :] = whole[g]
         mine[1, g : g + 1, :] = leave[g]
     carry_send(p, count, reach, 1, mine, inbox, cs, cr)
-    slot(6)
+    lax.fori_loop(0, 4, project_y, 0)
+    save(by, o_by)
+    save(wby, o_wby)
+    g_m[0].stage(3)
+    g_m[1].stage(1)
+    g_m[2].stage(0)
     carry_wait(p, count, reach, 1, mine, inbox, cs, cr)
     enter = carry_fold(p, count, reach, 1, inbox)
     inside, _ = chain(ends, enter, False)
@@ -502,55 +551,81 @@
     step = rows // SEG
 
     def states(g, c):
+        inside_g = hin[g]
         for s in range(SEG):
             lo = s * step
-            st = dr[g, lo + 8 : lo + 8 + step, :] + pq[g, lo : lo + step, :] * hin[g, s : s + 1, :]
+            st = dr[g, lo + 8 : lo + 8 + step, :] + pq[g, lo : lo + step, :] * segment_rows(inside_g, s, step)
             dr[g, lo + 8 : lo + 8 + step, :] = st
             mixed[g, lo : lo + step, :] = (st * gelu(by[g, lo : lo + step, :])).astype(BF16)
         return c
 
     lax.fori_loop(0, 8, states, 0)
-    saved.append(save(dr, o_st))
-    save(mixed, o_mixed)
+    saved.append(save(dr.at[:, 0 : rows + 8], o_st))
+    saved.append(save(mixed, o_mixed))
+    g_out.stage(4)
     save(wout, o_wout)
-    middle[...] = nt(wide(mixed, 4, 0, rows), chips(wout[0])) + nt(
+    for c in (saved_bx, saved_u1, saved_c):
+        c.wait()
+    middle = bx
+    v = nt(wide(mixed, 4, 0, rows), chips(wout[0])) + nt(
         jnp.concatenate([mixed[g] for g in range(4, 8)], axis=1), chips(wout[1])
     )
+
+    put(middle, v, 0, 0)
 
     def norm_two(r0):
         at = pl.ds(r0, 32)
-        m = middle[at, :] + tokens[at, :].astype(F32)
-        middle[at, :] = m
-        u2[at, :] = norm_rows(m, 1)
+        m = wide(middle, 6, r0, 32) + tokens[at, :].astype(F32)
+        for g in range(6):
+            middle[g, at, :] = m[:, g * 128 : (g + 1) * 128]
+        ubuf[at, :] = norm_rows(m, 1)
 
     rows_loop(rows, 32, norm_two)
+    g_m[0].stage(4)
+    g_m[2].stage(1)
     for c in saved:
         c.wait()
+    bufs = (m_r0, m_ra, m_rb, None, None, None)
+    red = [
+        Reduce(p, wm.at[k], wm, (k, p.core), bufs, ((k % 2,),) + tuple((k,) if k < n else None for n in (2, 1, 0, 0, 0)), rs.at[k],
+               rr.at[k])
+        for k in range(3)
+    ]
     fg, fu, fd, acc_out, acc_du = gx, ga, pq, sc, fac
+    hid, dgate = coded, mixed
 
     for k in range(3):
         if k > 0:
-            slot(6 + k)
+            g_m[k].stage(3)
+            g_m[k].stage(4)
         w0 = flat(wm[k, 0])
         w1 = flat(wm[k, 1])
         wg, wu, wd = w0[:, :768], jnp.concatenate([w0[:, 768:], w1[:, :384]], axis=1), w1[:, 384:]
-        put(fg, nt(u2[...], wg), 0, 0)
-        put(fu, nt(u2[...], wu), 0, 0)
+        put(fg, nt(ubuf[0:rows, :], wg), 0, 0)
+        put(fu, nt(ubuf[0:rows, :], wu), 0, 0)
         put(fd, nt(cot[...], wd), 0, 0)
 
         def glu(r0):
             at = pl.ds(r0, 32)
             for g in range(6):
-                cols = slice(g * 128, (g + 1) * 128)
                 act, slope = gelu_parts(fg[g, at, :])
                 up, dh = fu[g, at, :], fd[g, at, :]
-                hid[at, cols] = (act * up).astype(BF16)
-                dgate[at, cols] = (dh * up * slope).astype(BF16)
-                dup[at, cols] = (dh * act).astype(BF16)
+                hid[g, at, :] = (act * up).astype(BF16)
+                dgate[g, at, :] = (dh * up * slope).astype(BF16)
+                dup[g, at, :] = (dh * act).astype(BF16)
 
         rows_loop(rows, 32, glu)
-        v = nn(hid[...], wd)
-        v2 = nn(dgate[...], wg) + nn(dup[...], wu)
+        if k < 2:
+            g_m[k + 1].stage(2)
+        if k > 0:
+            red[0].stage(k)
+        if k == 1:
+            pl.semaphore_signal(free, inc=1, device_id=(p.pc,), device_id_type=MESH)
+        if k > 1:
+            red[1].stage(1)
+        v_hid, v_dg, v_dup = (wide(t, 6, 0, rows) for t in (hid, dgate, dup))
+        v = nn(v_hid, wd)
+        v2 = nn(v_dg, wg) + nn(v_dup, wu)
         for g in range(6):
             cols = slice(g * 128, (g + 1) * 128)
             if k == 0:
@@ -559,20 +634,22 @@
             else:
                 acc_out[g, 0:rows, :] += v[:, cols]
                 acc_du[g, 0:rows, :] += v2[:, cols]
-        gg = tn(dgate[...], u2[...]).astype(BF16)
-        gu = tn(dup[...], u2[...]).astype(BF16)
-        gd = tn(hid[...], cot[...]).astype(BF16)
+        gg = tn(v_dg, ubuf[0:rows, :]).astype(BF16)
+        gu = tn(v_dup, ubuf[0:rows, :]).astype(BF16)
+        gd = tn(v_hid, cot[...]).astype(BF16)
         wm[k, 0, :, :, :, 0:768] = gg.reshape(4, 4, 48, 768)
         wm[k, 0, :, :, :, 768:1152] = gu[:, :384].reshape(4, 4, 48, 384)
         wm[k, 1, :, :, :, 0:384] = gu[:, 384:].reshape(4, 4, 48, 384)
         wm[k, 1, :, :, :, 384:1152] = gd.reshape(4, 4, 48, 768)
-        save(wm.at[k], o_gm.at[k])
+        if k == 2:
+            pl.semaphore_wait(free, 1)
+        red[k].stage(0)
 
     o_gg2[...] = jnp.zeros_like(o_gg2)
 
     def finish(r0):
         at = pl.ds(r0, 32)
-        m, c = middle[at, :], cot[at, :].astype(F32)
+        m, c = wide(middle, 6, r0, 32), cot[at, :].astype(F32)
         out[at, :] = (m + wide(acc_out, 6, r0, 32)).astype(BF16)
         du = wide(acc_du, 6, r0, 32)
         inv = lax.rsqrt(jnp.mean(m * m, axis=1, keepdims=True) + EPSILON)
@@ -580,15 +657,25 @@
         gd_ = du * o_gain[1:2, :]
         back = jnp.mean(gd_ * m, axis=1, keepdims=True)
         dm = c + inv * gd_ - m * (inv * inv * inv * back)
-        hid[at, :] = dm.astype(BF16)
+        ubuf[at, :] = dm.astype(BF16)
         for g in range(6):
             acc_out[g, at, :] = dm[:, g * 128 : (g + 1) * 128]
 
     rows_loop(rows, 32, finish)
     save(acc_out.at[0:6], o_dmid)
-    save(hid, o_db)
+    save(ubuf.at[0:rows], o_db)
+    red[0].take(2)
+    save(wm.at[0, p.core, p.yx], o_part0)
+    red[2].take(0)
+    save(wm.at[2, p.core], o_part2)
+    red[1].take(1)
+    save(wm.at[1, p.core, p.yx], o_part1.at[0])
+    save(wm.at[1, p.core, p.gb], o_part1.at[1])
+    red[0].close(0, 1, 2, 3)
+    red[1].close(0, 1, 2)
+    red[2].close(0)
     for c in outs:
-        if not any(c is s for s in saved):
+        if not any(c is s for s in saved + [saved_bx, saved_u1, saved_c]):
             c.wait()
 
 
@@ -602,10 +689,10 @@
         (S((8, 8, 128), F32), VM),
         (S((8, width), F32), VM),
         (S((8, width), F32), VM),
-        (S((2, 4, 4, 48, 1024), BF16), ANY),
+        (S((2, 4, 4, 48, 512), BF16), ANY),
+        (S((2, 4, 4, 48, 512), BF16), ANY),
         (S((2, 4, 4, 64, 256), BF16), ANY),
         (S((2, 4, 4, 48, 512), BF16), ANY),
-        (S((3, 2, 4, 4, 48, 1152), BF16), ANY),
         (S(page, F32), ANY),
         (S(page, F32), ANY),
         (S(page, F32), ANY),
@@ -618,37 +705,38 @@
         (S((rows, width), BF16), ANY),
         (S((6, rows, 128), F32), ANY),
         (S((rows, width), BF16), ANY),
+        (S((4, 48, 1152), BF16), ANY),
+        (S((2, 4, 48, 1152), BF16), ANY),
+        (S((4, 4, 48, 1152), BF16), ANY),
     ]
     V = pltpu.VMEM
     dma = pltpu.SemaphoreType.DMA
     scratch = [
         V((2, 4, 4, 16, 128), BF16),
-        V((2, 4, 4, 48, 1024), BF16),
+        V((2, 4, 4, 48, 512), BF16),
+        V((2, 4, 4, 48, 512), BF16),
         V((2, 4, 4, 64, 256), BF16),
         V((2, 4, 4, 48, 512), BF16),
         V((3, 2, 4, 4, 48, 1152), BF16),
         V((8, rows + 16, 128), F32),
         V(page, F32),
-        V(page, F32),
-        V((8, rows + 8, 128), F32),
-        V(page, F32),
+        V((8, rows + PAD, 128), F32),
+        V((8, rows + 8 + PAD, 128), F32),
+        V((8, rows + PAD, 128), F32),
         V(page, F32),
         V(page, F32),
         V(page, F32),
         V((rows + 16, width), BF16),
         V(page, BF16),
         V(page, BF16),
-        V((rows, width), F32),
-        V((rows, width), BF16),
-        V((rows, 768), BF16),
-        V((rows, 768), BF16),
-        V((rows, 768), BF16),
+        V(page, BF16),
         V((rows, 128), jnp.int32),
+        V((8, 8, 128), F32),
         V((16, width), BF16),
         V((32, 128), F32),
         V((32, 128), F32),
-        V((2, 24, 1024), F32),
-        V((24, 1024), F32),
+        V((2, 2, 24, 512), F32),
+        V((2, 24, 512), F32),
         V((2, 24, 512), F32),
         V((24, 512), F32),
         V((2, 32, 256), F32),
@@ -658,15 +746,21 @@
         V((8, 8, 128), F32),
         V((2, 8, 128), F32),
         V((reach, 2, 8, 128), F32),
-        dma((7, 10)),
-        dma((7, 10)),
-        dma((5,)),
-        dma((5,)),
+        V((2, 4, 4, 48, 1152), BF16),
+        V((2, 2, 4, 48, 1152), BF16),
+        V((1, 4, 48, 1152), BF16),
+        dma((8, 10)),
+        dma((8, 10)),
+        dma((6,)),
+        dma((6,)),
         dma((1,)),
         dma((1,)),
         dma((reach,)),
         dma((reach,)),
-        dma((18,)),
+        dma((3, 8)),
+        dma((3, 8)),
+        dma((20,)),
+        pltpu.SemaphoreType.REGULAR,
     ]
     return pl.pallas_call(
         functools.partial(forward_kernel, count, reach),
@@ -683,76 +777,92 @@
 
 
 class Reduce:
-    def __init__(self, p, part, own, own_lead, bufs, lead, ssem, rsem, load=None):
-        self.p, self.part, self.load = p, part, load
-        self.whole, self.own_lead, self.bufs, self.lead = own, own_lead, bufs, lead
-        self.own = own.at[own_lead]
-        self.r0, self.ra, self.rb, self.rz, self.tot, self.rc = [b.at[lead] if lead else b for b in bufs]
+    def __init__(self, p, part, whole, own_lead, bufs, leads, ssem, rsem, groups=None):
+        self.p, self.part = p, part
+        self.whole, self.own_lead, self.bufs, self.leads = whole, own_lead, bufs, leads
         self.ssem, self.rsem = ssem, rsem
+        self.gyx, self.gb = groups or (p.yx, p.gb)
+
+    def own(self, *index):
+        return self.whole.at[self.own_lead + index]
+
+    def buf(self, which, *index):
+        at = self.leads[which] + index
+        return self.bufs[which].at[at] if at else self.bufs[which]
 
     def copy(self, slot):
-        p, own = self.p, self.own
+        p = self.p
         src, dst, dev = (
-            (lambda: (self.part.at[p.other], self.r0, p.pc)),
-            (lambda: (own.at[p.gd], self.ra.at[1], p.pa)),
-            (lambda: (own.at[p.ga], self.ra.at[0], p.pa)),
-            (lambda: (own.at[p.gb], self.rb, p.pb)),
-            (lambda: (own.at[p.yx, p.zs[0]], self.rz.at[0], p.pz[0])),
-            (lambda: (own.at[p.yx, p.zs[1]], self.rz.at[1], p.pz[1])),
-            (lambda: (own.at[p.yx, p.zs[2]], self.rz.at[2], p.pz[2])),
-            (lambda: (self.tot.at[p.other], self.rc, p.pc)),
+            (lambda: (self.part.at[p.other], self.buf(0), p.pc)),
+            (lambda: (self.own(p.gd), self.buf(1, 1), p.pa)),
+            (lambda: (self.own(p.ga), self.buf(1, 0), p.pa)),
+            (lambda: (self.own(self.gb), self.buf(2), p.pb)),
+            (lambda: (self.own(self.gyx, p.zs[0]), self.buf(3, 0), p.pz[0])),
+            (lambda: (self.own(self.gyx, p.zs[1]), self.buf(3, 1), p.pz[1])),
+            (lambda: (self.own(self.gyx, p.zs[2]), self.buf(3, 2), p.pz[2])),
+            (lambda: (self.buf(4, p.other), self.buf(5), p.pc)),
         )[slot]()
         return remote(src, dst, self.ssem.at[slot], self.rsem.at[slot], dev)
 
     def add(self, group, which, *index):
-        buf = self.bufs[which]
         for z in range(4):
             at = self.own_lead + (group, z)
-            other = buf[self.lead + index + (z,)]
+            other = self.bufs[which][self.leads[which] + index + (z,)]
             self.whole[at] = (self.whole[at].astype(F32) + other.astype(F32)).astype(BF16)
 
-    def stage(self, n):
+    def take(self, n, send=False):
         p = self.p
         if n == 0:
-            self.copy(0).start()
-            if self.load is not None:
-                self.load.start()
-        elif n == 1:
-            if self.load is not None:
-                self.load.wait()
             self.copy(0).wait_recv()
             for group, slot in ((p.gd, 1), (p.ga, 2)):
                 self.add(group, 0, group)
-                self.copy(slot).start()
-            for group in (p.gb, p.yx):
+                if send:
+                    self.copy(slot).start()
+            for group in (self.gb, self.gyx):
                 self.add(group, 0, group)
+        elif n == 1:
+            self.copy(1).wait_recv()
+            self.add(self.gb, 1, 1)
+            if send:
+                self.copy(3).start()
+            self.copy(2).wait_recv()
+            self.add(self.gyx, 1, 0)
         elif n == 2:
-            self.copy(1).wait_recv()
-            self.add(p.gb, 1, 1)
-            self.copy(3).start()
-            self.copy(2).wait_recv()
-            self.add(p.yx, 1, 0)
+            self.copy(3).wait_recv()
+            self.add(self.gyx, 2)
+            if send:
+                self.send(3)
         elif n == 3:
-            self.copy(3).wait_recv()
-            self.add(p.yx, 2)
-            for s in (4, 5, 6):
-                self.copy(s).start()
-        elif n == 4:
-            total = self.whole[self.own_lead + (p.yx, p.z)].astype(F32)
+            total = self.whole[self.own_lead + (self.gyx, p.z)].astype(F32)
             for d in range(3):
                 self.copy(4 + d).wait_recv()
-                total = total + self.bufs[3][self.lead + (d,)].astype(F32)
+                total = total + self.bufs[3][self.leads[3] + (d,)].astype(F32)
             half = total.shape[0] // 2
-            self.bufs[4][self.lead + (0,)] = total[:half]
-            self.bufs[4][self.lead + (1,)] = total[half:]
-            self.copy(7).start()
+            self.bufs[4][self.leads[4] + (0,)] = total[:half]
+            self.bufs[4][self.leads[4] + (1,)] = total[half:]
+            if send:
+                self.send(4)
+
+    def send(self, n):
+        for slot in ((0,), (1, 2), (3,), (4, 5, 6), (7,))[n]:
+            self.copy(slot).start()
+
+    def close(self, *slots):
+        for s in slots:
+            self.copy(s).wait_send()
+
+    def stage(self, n, first=0):
+        if n == 0:
+            self.send(0)
+        elif n < 5:
+            self.take(n - 1, True)
         else:
+            p = self.p
             self.copy(7).wait_recv()
-            mine, theirs = self.bufs[4][self.lead + (p.core,)], self.bufs[5][self.lead + (...,)]
+            mine, theirs = self.bufs[4][self.leads[4] + (p.core,)], self.bufs[5][self.leads[5] + (...,)]
             left = jnp.where(p.core == 0, mine, theirs)
             right = jnp.where(p.core == 0, theirs, mine)
-            for s in range(8):
-                self.copy(s).wait_send()
+            self.close(*range(first, 8))
             return left, right
 
 
@@ -787,12 +897,12 @@
 
 
 def backward_kernel(count, reach, *refs):
-    (tokens, lengths, par, gain, gg2, i_wproj, i_wgate, i_wout, i_gm, i_by, i_fac, i_gx, i_ga, i_sc, i_st, i_bx, i_coded,
-     i_mixed, i_u1, i_dmid, i_db,
+    (tokens, lengths, par, gain, gg2, i_wbx, i_wby, i_wgate, i_wout, i_by, i_fac, i_gx, i_ga, i_sc, i_st, i_bx, i_coded,
+     i_mixed, i_u1, i_dmid, i_db, i_part0, i_part1, i_part2,
      grad_tokens, o_proj, o_out, o_gate, o_in, o_down, o_cw, o_cb, o_gb, o_dec, o_g1, o_g2,
-     wproj, wgate, wout, adj, fac, st, pp, gslot, coded, mixed, u1, db, dby, dgx, since,
-     own_m, gout, gpy, gpx, ggate,
-     m_r0, m_ra, m_rb, m_rz, m_tot, m_rc, p_r0, p_ra, p_rb, p_rz, p_tot, p_rc, t_r0, t_ra, t_rb, t_rz, t_tot, t_rc,
+     wbx, wby, wgate, wout, adj, fac, st, pp, gslot, coded, mixed, u1, db, dby, dgx, since,
+     own0, own1, own2, gout, gpy, gpx, ggate,
+     m_ra, m_rb, m_rz, m_tot, m_rc, p_r0, p_ra, p_rb, p_rz, p_tot, p_rc, t_r0, t_ra, t_rb, t_rz, t_tot, t_rc,
      edge, sums, gsum, vsum, vbuf, hin, mine, inbox,
      rs, rr, vs, vr, cs, cr, es, er, isem, gsem, lsem) = refs
     p = Place()
@@ -803,25 +913,31 @@
     edge[...] = jnp.zeros_like(edge)
     entry_barrier(p, count, reach)
 
+    mbufs = (None, m_ra, m_rb, m_rz, m_tot, m_rc)
     red_m = [
-        Reduce(p, i_gm.at[k], own_m, (k,), (m_r0, m_ra, m_rb, m_rz, m_tot, m_rc), (k,), rs.at[k], rr.at[k],
-               pltpu.make_async_copy(i_gm.at[k, p.core], own_m.at[k], lsem.at[k]))
-        for k in range(3)
+        Reduce(p, None, own, (), mbufs, (None, (), (max(k - 1, 0),), (k,), (k,), (k,)), rs.at[k], rr.at[k], groups)
+        for k, own, groups in ((0, own0, (0, None)), (1, own1, (0, 1)), (2, own2, None))
     ]
     pbufs = (p_r0, p_ra, p_rb, p_rz, p_tot, p_rc)
     red_out, red_py, red_px = [
-        Reduce(p, g, g, (p.core,), pbufs, (k,), rs.at[3 + k], rr.at[3 + k])
-        for k, g in enumerate((gout, gpy, gpx))
+        Reduce(p, g, g, (p.core,), pbufs, ((k,),) * 6, rs.at[3 + k], rr.at[3 + k]) for k, g in enumerate((gout, gpy, gpx))
     ]
-    red_gate = Reduce(p, ggate, ggate, (p.core,), (t_r0, t_ra, t_rb, t_rz, t_tot, t_rc), (), rs.at[6], rr.at[6])
-
-    for r in red_m:
-        r.stage(0)
+    red_gate = Reduce(
+        p, ggate, ggate, (p.core,), (t_r0, t_ra, t_rb, t_rz, t_tot, t_rc), ((),) * 6, rs.at[6], rr.at[6]
+    )
+
+    parts = [
+        pltpu.make_async_copy(i_part0, own0.at[0], lsem.at[0]),
+        pltpu.make_async_copy(i_part1, own1, lsem.at[1]),
+        pltpu.make_async_copy(i_part2, own2, lsem.at[2]),
+    ]
+    for c in parts:
+        c.start()
     loads = {}
     for i, (name, src, dst) in enumerate((
         ("db", i_db, db), ("wout", i_wout, wout), ("by", i_by, adj.at[:, 0:rows]), ("st", i_st, st), ("mixed", i_mixed, mixed),
-        ("u1", i_u1, u1), ("fac", i_fac, fac), ("coded", i_coded, coded), ("wgate", i_wgate, wgate),
-        ("wproj", i_wproj, wproj))):
+        ("u1", i_u1, u1), ("fac", i_fac, fac.at[:, 0:rows]), ("coded", i_coded, coded), ("wgate", i_wgate, wgate),
+        ("wby", i_wby, wby), ("wbx", i_wbx, wbx))):
         loads[name] = pltpu.make_async_copy(src, dst, isem.at[i])
         loads[name].start()
 
@@ -840,19 +956,24 @@
     sums[...] = jnp.zeros_like(sums)
     gsum[...] = jnp.zeros_like(gsum)
 
+    parts[0].wait()
+    red_m[0].send(3)
+    parts[1].wait()
+    red_m[1].send(2)
+    parts[2].wait()
+    red_m[2].send(1)
     loads["db"].wait()
     loads["wout"].wait()
 
     def mix_dots(h, c):
         cols = pl.ds(pl.multiple_of(lax.rem(h, 2) * 256, 256), 256)
         v = nn(db[...], chips(wout[lax.div(h, 2), :, :, :, cols]))
-        pp[2 * h], pp[2 * h + 1] = v[:, :128], v[:, 128:]
+        pp[2 * h, 0:rows, :], pp[2 * h + 1, 0:rows, :] = v[:, :128], v[:, 128:]
         return c
 
     lax.fori_loop(0, 4, mix_dots, 0)
     loads["by"].wait()
     loads["st"].wait()
-    red_m[0].stage(1)
 
     def branch_y(g, r0):
         at = pl.ds(r0, 64)
@@ -862,31 +983,31 @@
         dby[g, at, :] = (dm * st[g, pl.ds(r0 + 8, 64), :] * slope).astype(BF16)
 
     blocks_loop(8, rows, 64, branch_y)
-    red_m[1].stage(1)
-    loads["mixed"].wait()
-
-    def halves(target, left, page):
-        for h in range(2):
-            v = tn(left, jnp.concatenate([page[4 * h + i] for i in range(4)], axis=1))
-            put_chips(target, h, v.astype(BF16))
-
-    halves(gout, db[...], mixed)
-    red_out.stage(0)
-    red_m[2].stage(1)
-    loads["u1"].wait()
-    halves(gpy, u1[...], dby)
-    red_py.stage(0)
-    red_m[0].stage(2)
     loads["fac"].wait()
-    ends = scan_segments(rows, fac, adj, pp, 0, 0, 0, True)
+    fac[:, rows:, :] = jnp.ones((8, PAD, 128), F32)
+    adj[:, rows:, :] = jnp.zeros((8, PAD, 128), F32)
+    ends = scan_segments(fac, adj, pp, 0, 0, 0, True)
     _, leave = chain(ends, [jnp.zeros((1, 128), F32)] * 8, True)
     whole = products(ends)
     for g in range(8):
         mine[0, g : g + 1, :] = whole[g]
         mine[1, g : g + 1, :] = leave[g]
     carry_send(p, count, reach, -1, mine, inbox, cs, cr)
-    red_out.stage(1)
-    red_m[0].stage(3)
+    red_m[1].stage(3)
+    loads["mixed"].wait()
+
+    def halves(target, left, page):
+        for h in range(2):
+            v = tn(left, jnp.concatenate([page[4 * h + i] for i in range(4)], axis=1))
+            put_chips(target, h, v.astype(BF16))
+
+    halves(gout, db[...], mixed)
+    red_out.stage(0)
+    loads["u1"].wait()
+    halves(gpy, u1[...], dby)
+    red_py.stage(0)
+    red_m[0].stage(4)
+    red_m[2].stage(2)
     carry_wait(p, count, reach, -1, mine, inbox, cs, cr)
     inside, _ = chain(ends, carry_fold(p, count, reach, -1, inbox), True)
     for g in range(8):
@@ -894,13 +1015,14 @@
     step = rows // SEG
 
     def adjoint(g, c):
+        inside_g = hin[g]
         for s in range(SEG):
             lo = s * step
-            adj[g, lo : lo + step, :] += pp[g, lo : lo + step, :] * hin[g, s : s + 1, :]
+            adj[g, lo : lo + step, :] += pp[g, lo : lo + step, :] * segment_rows(inside_g, s, step)
         return c
 
     lax.fori_loop(0, 8, adjoint, 0)
-    red_m[1].stage(2)
+    red_out.stage(1)
     red_py.stage(1)
     loads["coded"].wait()
     dga = mixed
@@ -942,12 +1064,12 @@
 
     pairs_loop(gate_back)
     fetch_bx(0, 0).start()
-    load_dmid = pltpu.make_async_copy(i_dmid, st.at[0:6, 0:rows], isem.at[10])
+    load_dmid = pltpu.make_async_copy(i_dmid, st.at[0:6, 0:rows], isem.at[11])
     load_dmid.start()
     dbx = dgx
-    red_m[2].stage(2)
-    red_m[1].stage(3)
-    red_m[0].stage(4)
+    red_m[2].stage(3)
+    red_m[1].stage(4)
+    red_out.stage(2)
     loads["wgate"].wait()
 
     def gate_dots(h, c):
@@ -968,10 +1090,11 @@
     def _():
         to_prev.start()
 
-    red_out.stage(2)
-    red_m[2].stage(3)
     red_py.stage(2)
-    red_m[1].stage(4)
+    loads["wby"].wait()
+    put(pp, nt(jnp.concatenate([dby[g] for g in range(8)], axis=1), whole_w(wby)), 0, 0)
+    red_out.stage(3)
+    red_m[2].stage(4)
 
     @pl.when(me > 0)
     def _():
@@ -1014,19 +1137,15 @@
     halves(gpx, u1[...], dbx)
     red_px.stage(0)
     red_gate.stage(1)
-    red_out.stage(3)
     red_py.stage(3)
-    red_m[2].stage(4)
-    loads["wproj"].wait()
-    du = nt(jnp.concatenate([dbx[g] for g in range(8)], axis=1), chips(wproj[0])) + nt(
-        jnp.concatenate([dby[g] for g in range(8)], axis=1), chips(wproj[1])
-    )
-    put(pp, du, 0, 0)
+    loads["wbx"].wait()
+    du = nt(jnp.concatenate([dbx[g] for g in range(8)], axis=1), whole_w(wbx))
+    for g in range(6):
+        pp[g, 0:rows, :] += du[:, g * 128 : (g + 1) * 128]
     red_px.stage(1)
     red_gate.stage(2)
     red_out.stage(4)
     red_py.stage(4)
-
     load_dmid.wait()
 
     def finish(r0):
@@ -1058,7 +1177,7 @@
     tot.stage(3)
     red_gate.stage(4)
     for k in range(3):
-        left, right = red_m[k].stage(5)
+        left, right = red_m[k].stage(5, (4, 3, 1)[k])
         lo = 24 * k
         o_in[lo : lo + 24, 0:1152] = left
         o_in[lo : lo + 24, 1152:1536] = right[:, :384]
@@ -1102,29 +1221,29 @@
                 V(lead + (3, r, c), BF16), V(lead + (2, r // 2, c), F32), V(lead + (r // 2, c), F32)]
 
     scratch = [
-        V((2, 4, 4, 48, 1024), BF16), V((2, 4, 4, 64, 256), BF16), V((2, 4, 4, 48, 512), BF16),
+        V((2, 4, 4, 48, 512), BF16), V((2, 4, 4, 48, 512), BF16), V((2, 4, 4, 64, 256), BF16), V((2, 4, 4, 48, 512), BF16),
+        V((8, rows + PAD, 128), F32),
+        V((8, rows + PAD, 128), F32),
         V((8, rows + 8, 128), F32),
-        V(page, F32),
-        V((8, rows + 8, 128), F32),
-        V(page, F32),
+        V((8, rows + PAD, 128), F32),
         V((2, 3, rows + 16, 128), F32),
         V(page, BF16), V(page, BF16), V((rows, width), BF16), V((rows, width), BF16),
         V(page, BF16), V(page, BF16),
         V((rows + 8, 128), jnp.int32),
-        V((3, 4, 4, 48, 1152), BF16),
+        V((1, 4, 48, 1152), BF16), V((2, 4, 48, 1152), BF16), V((4, 4, 48, 1152), BF16),
         V((2, 4, 4, 48, 512), BF16), V((2, 4, 4, 48, 512), BF16), V((2, 4, 4, 48, 512), BF16),
         V((2, 4, 4, 64, 256), BF16),
-        *bufs(3, 48, 1152), *bufs(3, 48, 512), *bufs(0, 64, 256),
+        V((2, 4, 48, 1152), BF16), V((2, 4, 48, 1152), BF16), *bufs(3, 48, 1152)[3:], *bufs(3, 48, 512), *bufs(0, 64, 256),
         V((2, 8, 8, 128), F32),
         V((8, 8, 128), F32), V((8, width), F32), V((4, 16, 1024), F32), V((6, 16, 1024), F32),
         V((8, 8, 128), F32), V((2, 8, 128), F32), V((reach, 2, 8, 128), F32),
         dma((7, 8)), dma((7, 8)), dma((6,)), dma((6,)), dma((reach,)), dma((reach,)), dma((1,)), dma((1,)),
-        dma((11,)), dma((2, 4)), dma((3,)),
+        dma((12,)), dma((2, 4)), dma((3,)),
     ]
     return pl.pallas_call(
         functools.partial(backward_kernel, count, reach),
         out_shape=outs,
-        in_specs=[VM, SM, VM, VM, VM] + [ANY] * 16,
+        in_specs=[VM, SM, VM, VM, VM] + [ANY] * 19,
         out_specs=[VM] * len(outs),
         scratch_shapes=scratch,
         name="backward",
@@ -1133,6 +1252,23 @@
             collective_id=1, has_side_effects=True, vmem_limit_bytes=63 * MIB
         ),
     )(*args)
+
+
+def results_kernel(n, *refs):
+    for i in range(n):
+        refs[n + i][...] = refs[i][...]
+
+
+def results_call(arrays):
+    n = len(arrays)
+    return pl.pallas_call(
+        functools.partial(results_kernel, n),
+        out_shape=[jax.ShapeDtypeStruct(a.shape, a.dtype) for a in arrays],
+        in_specs=[VM] * n,
+        out_specs=[VM] * n,
+        name="results",
+        cost_estimate=pl.CostEstimate(flops=0, bytes_accessed=2 * sum(a.size * a.dtype.itemsize for a in arrays), transcendentals=0),
+    )(*arrays)
 
 
 def from_behind(x, axis, by):
@@ -1406,14 +1542,19 @@
     rows = tokens.shape[0]
     longest = rows * count // 12
     reach = -(-(longest - 1) // rows)
-    (output, par, gain, gg2, wproj, wgate, wout, gm, by, fac, gx, ga, sc, st, bx, coded, mixed, u1, dmid, db) = forward_call(
+    (output, par, gain, gg2, wbx, wby, wgate, wout, by, fac, gx, ga, sc, st, bx, coded, mixed, u1, dmid, db, part0, part1,
+     part2) = forward_call(
         count, reach,
         (tokens, cotangent, lengths, conv_weight, conv_bias[None], gate_bias, decay_param[None], gain_norm1[None],
          gain_norm2[None], proj_in, out_proj, gate_blocks, mlp_in, mlp_down),
     )
-    (grad_tokens, g_proj, g_out, g_gate, g_in, g_down, g_cw, g_cb, g_gb, g_dec, g_n1, g_n2) = backward_call(
+    grads = backward_call(
         count, reach,
-        (tokens, lengths, par, gain, gg2, wproj, wgate, wout, gm, by, fac, gx, ga, sc, st, bx, coded, mixed, u1, dmid, db),
+        (tokens, lengths, par, gain, gg2, wbx, wby, wgate, wout, by, fac, gx, ga, sc, st, bx, coded, mixed, u1, dmid, db,
+         part0, part1, part2),
+    )
+    (output, grad_tokens, g_proj, g_out, g_gate, g_in, g_down, g_cw, g_cb, g_gb, g_dec, g_n1, g_n2) = results_call(
+        [output, *grads]
     )
     return (
         output, grad_tokens, g_n1[0], g_n2[0], g_proj, g_out, g_gate, g_cw, g_cb[0], g_gb, g_dec[0], g_in, g_down,

time: 269 us -> 228 us (0.85); the launches traced: 264 us -> 228 us
  Pallas kernels: 252 us -> 227 us
  local copies, waits for them, and re-layouts: 10.1 us -> 0 us
    pallas_call x1, Pallas kernels: 122 us -> 90.4 us  [backward_call(): pl.pallas_call(functools.partial(backward_kernel, count, reach), out_shap...]
    unnamed x37 -> x0, local copies, waits for them, and re-layouts: 10.1 us -> none
    pallas_call x0 -> x1, Pallas kernels: none -> 3.75 us  [results_call(): pl.pallas_call(functools.partial(results_kernel, n), out_shape=[jax.Shape...]
where the time goes in v2:
time: 228 us
  Pallas kernels  227 us (100%)
    pallas_call x1, Pallas kernels, forward_call(): pl.pallas_call(functools.partial(forward_kernel, count, reach), out_shape...  133 us
    pallas_call x1, Pallas kernels, backward_call(): pl.pallas_call(functools.partial(backward_kernel, count, reach), out_shap...  90.4 us

profile of v2, /device:TPU:0, one launch (start us, length us, event | category | flops | bytes accessed | tf_op | source)
XLA Modules:
  0.0 227.6 jit_solution(17615793404992019891)
XLA Ops:
  0.6 132.6 %forward.1 = (bf16[768,768]{1,0:T(8,128)(2,1)}, f32[8,8,128]{2,1,0:T(8,128)}, f32[8,768]{1,0:T(8,128)}, f32[8,768]{1,0:T(8,128)}, bf16[2,4,4,48,512]{4,3,2,1,0:T...) custom-call(bf16[768,768]{1,0:T(8,128)(2,1)} %refs_0_.3, ...), custom_call_target="tpu_custom_call" | custom-call | flops 24999999488 | bytes 60000000 | tf_op jit(solution)/shard_map/forward/pallas_call | solution.py:765
  133.3 90.4 %backward.1 = (bf16[768,768]{1,0:T(8,128)(2,1)}, f32[24,2048]{1,0:T(8,128)}, f32[24,1024]{1,0:T(8,128)}, f32[32,512]{1,0:T(8,128)}, f32[72,1536]{1,0:T(8,128)}, ...) custom-call(bf16[768,768]{1,0:T(8,128)(2,1)} %refs_0_.3, ...), custom_call_target="tpu_custom_call" | custom-call | flops 12000000000 | bytes 60000000 | tf_op jit(solution)/shard_map/backward/pallas_call | solution.py:1243
  223.7 3.8 %results.1 = (bf16[768,768]{1,0:T(8,128)(2,1)}, bf16[768,768]{1,0:T(8,128)(2,1)}, f32[24,2048]{1,0:T(8,128)}, f32[24,1024]{1,0:T(8,128)}, f32[32,512]{1,0:T(8,12...) custom-call(bf16[768,768]{1,0:T(8,128)(2,1)} %get-tuple-element.61.r, ...), custom_call_target="tpu_custom_call" | custom-call | bytes 6769024 | tf_op jit(solution)/shard_map/results/pallas_call | solution.py:1264
